TPU v7x, 512 devices: a whole 4x8x8 slice. The times are simulated.
512 devices in a mesh: pool: 32 (over z, x), tp: 16 (over y, core).
Axes of the slice: x: 4, y: 8, z: 8, core: 2. Of those that a mesh axis runs over, the one named last changes fastest.
Arguments:
- pool_kv: bfloat16 [2048, 2, 1024, 128], P('pool', None, 'tp'), may hold values from -6 to 6
- queries: bfloat16 [64, 128, 8192], P('pool', None, 'tp'), may hold values from -9 to 9
- new_kv: bfloat16 [64, 2, 1024, 128], P('pool', None, 'tp'), may hold values from -9 to 9
- page_table: int32 [64, 32], replicated, may hold values from -1 to 2047, as said below
- prefix_pages: int32 [64], replicated, may hold values from 8 to 32, as said below
Outputs:
- attended: bfloat16 [64, 128, 8192], P('pool', None, 'tp')
- landed: bfloat16 [64, 2, 1024, 128], P('pool', None, 'tp')
Inputs may be any that keep to these rules, and one draw needn't show every extreme that they name: `page_table`: entry j < prefix_pages[r] of row r is owner * 64 + slot, the owner being the pool index that holds the page; later entries are -1. The pages of one request lie on distinct owners, so an owner holds at most one page of each request; no slot holds two pages. `prefix_pages`: some request has a prefix of 32 pages.
All inputs are finite; a program needn't handle non-finite values.
Results may differ from a plain program's by a relative error of at most 0.0052.
Values may be sent and summed in bfloat16 or wider, within the bound.
No kernel may reach another device: no remote copies, remote signals or barrier semaphores. Data moves between devices by JAX's collectives and lax.ppermute only.
A program may use at most 64 MiB of HBM per device.

v0:
```python
import math

import jax
import jax.numpy as jnp
from jax import lax
from jax.sharding import PartitionSpec as P


def partner_2(value, axis, distance):
    mask = 2**distance
    pairs = [(source, source ^ mask) for source in range(lax.axis_size(axis))]
    return lax.ppermute(value, axis, pairs)


def from_behind(array, axis, by):
    devices = lax.axis_size(axis)
    return lax.ppermute(array, axis, [(i, (i + by) % devices) for i in range(devices)])


def rope_tables(positions, head_width):
    indices = jnp.arange(head_width // 2, dtype=jnp.float32)
    inverse = jnp.power(jnp.float32(1000000.0), -2.0 * indices / head_width)
    angles = positions.astype(jnp.float32)[:, None] * inverse[None, :]
    angles = jnp.concatenate([angles, angles], axis=1)
    return (jnp.cos(angles), jnp.sin(angles))


def rotate(values, cosine_table, sine_table):
    half_size = values.shape[-1] // 2
    turned = jnp.concatenate([-values[..., half_size:], values[..., :half_size]], axis=-1)
    return values * cosine_table + turned * sine_table


def joined(mine, partner, lower_half):
    return jnp.where(
        lower_half,
        jnp.concatenate([mine, partner], axis=-2),
        jnp.concatenate([partner, mine], axis=-2),
    )


def on_device(pool_kv, queries, new_kv, page_table, prefix_pages):
    pool_count = lax.axis_size("pool")
    pool_rank = lax.axis_index("pool")
    lower_half = lax.axis_index("tp") % 2 == 0
    slot_count = pool_kv.shape[0]
    half_width = pool_kv.shape[2]
    page_len = pool_kv.shape[3]
    head_width = 2 * half_width
    local_requests = queries.shape[0]
    suffix_len = queries.shape[1]
    head_count = queries.shape[2] // head_width
    page_spots = jnp.arange(page_table.shape[1], dtype=jnp.int32)
    owner_of = jnp.where(page_spots[None, :] < prefix_pages[:, None], page_table // slot_count, -1)
    slot_of = jnp.sum(jnp.where(owner_of == pool_rank, page_table % slot_count, 0), axis=1)
    first_row = pool_rank * local_requests
    own_owners = lax.dynamic_slice_in_dim(owner_of, first_row, local_requests, 0)
    own_lengths = lax.dynamic_slice_in_dim(prefix_pages, first_row, local_requests, 0)
    owner_ids = jnp.arange(pool_count, dtype=jnp.int32)
    present = jnp.any(own_owners[None, :, :] == owner_ids[:, None, None], axis=2)
    other_pool, other_fresh = partner_2((pool_kv, new_kv), "tp", 0)
    whole_pool = joined(pool_kv, other_pool, lower_half)
    outgoing = whole_pool[slot_of].reshape(pool_count, local_requests, 2, head_width, page_len)
    arrived = lax.all_to_all(outgoing, "pool", split_axis=0, concat_axis=0, tiled=True)
    fresh_kv = joined(new_kv, other_fresh, lower_half)
    score_scale = 1.0 / math.sqrt(head_width)
    row_count = suffix_len * head_count
    prefix_keys = pool_count * page_len
    row_token = jnp.arange(row_count, dtype=jnp.int32) // head_count
    causal = jnp.arange(suffix_len, dtype=jnp.int32)[None, :] <= row_token[:, None]
    contract_last = (((1,), (1,)), ((), ()))
    results = []
    landing = []
    for request in range(local_requests):
        positions = own_lengths[request] * page_len + jnp.arange(suffix_len, dtype=jnp.int32)
        cosine_table, sine_table = rope_tables(positions, head_width)
        query_heads = (
            queries[request].reshape(suffix_len, head_count, head_width).astype(jnp.float32)
        )
        rotated_q = (
            rotate(query_heads, cosine_table[:, None, :], sine_table[:, None, :])
            .astype(jnp.bfloat16)
            .reshape(row_count, head_width)
        )
        rotated_k = rotate(
            fresh_kv[request, 0].T.astype(jnp.float32), cosine_table, sine_table
        ).astype(jnp.bfloat16)
        page_scores = jnp.einsum(
            "rd,odp->rop", rotated_q, arrived[:, request, 0], preferred_element_type=jnp.float32
        ).reshape(row_count, prefix_keys)
        own_scores = lax.dot_general(
            rotated_q, rotated_k, contract_last, preferred_element_type=jnp.float32
        )
        scores = jnp.concatenate([page_scores, own_scores], axis=1) * score_scale
        live_keys = jnp.repeat(present[:, request], page_len)
        allowed = jnp.concatenate(
            [jnp.broadcast_to(live_keys[None, :], (row_count, prefix_keys)), causal], axis=1
        )
        scores = jnp.where(allowed, scores, -jnp.inf)
        largest = jnp.max(scores, axis=1, keepdims=True)
        weights = jnp.exp(scores - largest)
        totals = jnp.sum(weights, axis=1, keepdims=True)
        rounded = weights.astype(jnp.bfloat16)
        page_part = rounded[:, :prefix_keys].reshape(row_count, pool_count, page_len)
        summed = jnp.einsum(
            "rop,odp->rd", page_part, arrived[:, request, 1], preferred_element_type=jnp.float32
        )
        summed = summed + lax.dot_general(
            rounded[:, prefix_keys:],
            fresh_kv[request, 1],
            contract_last,
            preferred_element_type=jnp.float32,
        )
        results.append(
            (summed / totals).reshape(suffix_len, head_count * head_width).astype(jnp.bfloat16)
        )
        key_columns = rotated_k.T
        own_keys = jnp.where(lower_half, key_columns[:half_width], key_columns[half_width:])
        landing.append(jnp.stack([own_keys, new_kv[request, 1]], axis=0))
    landed = from_behind(jnp.stack(landing, axis=0), "pool", pool_count // 2)
    return (jnp.stack(results, axis=0), landed)


def solution(mesh):
    return jax.shard_map(
        on_device,
        mesh=mesh,
        in_specs=(
            P("pool", None, "tp", None),
            P("pool", None, "tp"),
            P("pool", None, "tp", None),
            P(),
            P(),
        ),
        out_specs=(P("pool", None, "tp"), P("pool", None, "tp", None)),
        check_vma=False,
    )
```

profile of v0, /device:TPU:35, one launch (start us, length us, event | category | flops | bytes accessed | tf_op | source)
XLA Modules:
  0.0 157.0 jit_solution(2197706243744424005)
XLA Ops:
  0.6 2.6 %collective-permute-start = (bf16[64,2,64,128]{3,2,1,0:T(8,128)(2,1)}, bf16[64,2,64,128]{3,2,1,0:T(8,128)(2,1)S(1)}, u32[]{:S(2)}, u32[]{:S(2)}) collective-permute-start(bf16[64,2,64,128]{3,2,1,0:T(8,128)(2,1)} %param.5), channel_id=1, source_target_pairs={{0,1},{1,0},{2,3},{3,2},{4,5},{5,4},{6,7},{7,6},{8,9},{9,8},{10,11... | collective-permute-start | bytes 6291464 | tf_op jit(solution)/shard_map/ppermute | solution.py:12
  3.2 0.8 fusion.47
  4.0 3.2 %collective-permute-done = bf16[64,2,64,128]{3,2,1,0:T(8,128)(2,1)S(1)} collective-permute-done((bf16[64,2,64,128]{3,2,1,0:T(8,128)(2,1)}, bf16[64,2,64,128]{3,2,1,0:T(8,128)(2,1)S(1)}, u32[]{:S(2)}, u32[]{:S(2)}) %collective-permute-start) | collective-permute-done | bytes 2097184 | tf_op jit(solution)/shard_map/ppermute | solution.py:12
  7.2 5.3 %maximum_select_fusion = bf16[64,2,128,128]{3,2,1,0:T(8,128)(2,1)} fusion(bf16[64,2,64,128]{3,2,1,0:T(8,128)(2,1)S(1)} %collective-permute-done, bf16[64,2,64,128]{3,2,1,0:T(8,128)(2,1)} %param.5, pred[]{:T(512)S(6)} %eq.29), kind=kLoop, calls=%fused_computation.21 | loop fusion | flops 18874368 | bytes 8388609 | tf_op jit(solution)/shard_map/jit(_where)/select_n | solution.py:35
  12.5 5.2 %gather_fusion = bf16[64,2,128,128]{3,2,1,0:T(8,128)(2,1)} fusion(bf16[64,2,128,128]{3,2,1,0:T(8,128)(2,1)} %maximum_select_fusion, s32[1024]{0:T(1024)S(1)} %pad_clamp_fusion), kind=kCustom, calls=%fused_computation | custom fusion | bytes 8388864 | tf_op jit(solution)/shard_map/gather | solution.py:63
  17.7 13.1 %all-to-all-start = ((bf16[32,2,2,128,128]{4,3,2,1,0:T(8,128)(2,1)}), bf16[32,2,2,128,128]{4,3,2,1,0:T(8,128)(2,1)}, u32[]{:S(2)}, u32[]{:S(2)}) async-start(bf16[32,2,2,128,128]{4,3,2,1,0:T(8,128)(2,1)} %bitcast.115), calls=%async_computation | async-start | bytes 8388608 | tf_op jit(solution)/shard_map/all_to_all | solution.py:64
  30.8 2.8 %collective-permute-start.1 = (bf16[2,2,64,128]{3,2,1,0:T(8,128)(2,1)S(1)}, bf16[2,2,64,128]{3,2,1,0:T(8,128)(2,1)S(1)}, u32[]{:S(2)}, u32[]{:S(2)}) collective-permute-start(bf16[2,2,64,128]{3,2,1,0:T(8,128)(2,1)S(1)} %copy-done.6), channel_id=1, source_target_pairs={{0,1},{1,0},{2,3},{3,2},{4,5},{5,4},{6,7},{7,6},{8,9},{9,8},{10,11... | collective-permute-start | bytes 196616 | tf_op jit(solution)/shard_map/ppermute | solution.py:12
  33.7 0.6 fusion.61
  36.1 0.1 fusion.46
  36.3 0.8 iota_compare_fusion
  37.1 0.2 slice_negate_fusion.1
  37.3 0.2 slice_negate_fusion
  37.8 0.5 fusion.45
  38.7 7.2 %collective-permute-start.2 = (bf16[2,2,64,128]{3,2,1,0:T(8,128)(2,1)S(1)}, bf16[2,2,64,128]{3,2,1,0:T(8,128)(2,1)S(1)}, u32[]{:S(2)}, u32[]{:S(2)}) collective-permute-start(bf16[2,2,64,128]{3,2,1,0:T(8,128)(2,1)S(1)} %pad_maximum_fusion.3), channel_id=1, source_target_pairs={{0,256},{16,272},{32,288},{48,304},{64,320},{80,336},{96,352},{112... | collective-permute-start | bytes 196616 | tf_op jit(solution)/shard_map/ppermute | solution.py:17
  45.9 0.2 fusion.25
  46.3 0.3 fusion.34
  46.6 1.0 fusion.32
  47.6 0.9 fusion.29
  48.5 82.7 %collective-permute-done.2 = bf16[2,2,64,128]{3,2,1,0:T(8,128)(2,1)S(1)} collective-permute-done((bf16[2,2,64,128]{3,2,1,0:T(8,128)(2,1)S(1)}, bf16[2,2,64,128]{3,2,1,0:T(8,128)(2,1)S(1)}, u32[]{:S(2)}, u32[]{:S(2)}) %collective-permute-start.2) | collective-permute-done | bytes 65568 | tf_op jit(solution)/shard_map/ppermute | solution.py:17
  131.2 1.7 %fusion.60 = (bf16[32,1,1,128,128]{4,3,2,1,0:T(8,128)(2,1)S(1)}, bf16[32,1,1,128,128]{4,3,2,1,0:T(8,128)(2,1)S(1)}) fusion(bf16[32,2,2,128,128]{4,3,2,1,0:T(8,128)(2,1)} %all-to-all-done), kind=kLoop, calls=%fused_computation.122 | loop fusion | bytes 4194304 | tf_op jit(solution)/shard_map/slice | solution.py:89
  132.9 0.7 copy.58
  133.6 0.7 copy.56
  134.3 1.3 fusion.62
  135.6 1.3 fusion.63
  136.9 4.8 %fusion.13 = (f32[512]{0:T(512)S(1)}, f32[512]{0:T(512)S(1)}) fusion(f32[512,128]{1,0:T(8,128)S(1)} %fusion.34, f32[512,4096]{1,0:T(8,128)S(1)} %fusion.62, pred[512,128]{1,0:T(8,128)(4,1)S(1)} %copy-done.2, pred[4224]{0:T(1024)(128)(4,1)S(1)} %pad.38.clone, f32[512,128]{1,0:T(8,128)S(1)} %copy-done, f32[512,4096]{1,0:T(8,128)S(1)} %fusion.63, ...), kind=kLoop, calls=%fused_computation.23 | loop fusion | flops 21625856 | bytes 17379584 | tf_op jit(solution)/shard_map/reduce_max | solution.py:100
  141.7 6.1 %fusion.2 = (f32[512]{0:T(512)S(1)}, f32[512]{0:T(512)S(1)}, bf16[512,4224]{1,0:T(8,128)(2,1)}, bf16[512,4224]{1,0:T(8,128)(2,1)S(1)}) fusion(f32[512]{0:T(512)S(1)} %get-tuple-element.4, f32[512,128]{1,0:T(8,128)S(1)} %fusion.34, f32[512,4096]{1,0:T(8,128)S(1)} %fusion.62, pred[512,128]{1,0:T(8,128)(4,1)S(1)} %copy-done.2, ...), kind=kLoop, calls=%fused_computation.9 | loop fusion | flops 30276608 | bytes 26034432 | tf_op jit(solution)/shard_map/reduce_sum | solution.py:102
  147.8 2.5 %fusion.17 = f32[512,128]{1,0:T(8,128)S(1)} fusion(bf16[32,2,2,128,128]{4,3,2,1,0:T(8,128)(2,1)} %all-to-all-done, bf16[512,4224]{1,0:T(8,128)(2,1)S(1)} %get-tuple-element.7), kind=kOutput, calls=%fused_computation.25 | convolution fusion | flops 536870912 | bytes 5505024 | tf_op jit(solution)/shard_map/rop,odp->rd/dot_general | solution.py:105
  150.3 0.2 fusion.23
  150.7 3.8 %fusion.14 = f32[512,128]{1,0:T(8,128)S(1)} fusion(bf16[32,2,2,128,128]{4,3,2,1,0:T(8,128)(2,1)} %all-to-all-done, bf16[512,4224]{1,0:T(8,128)(2,1)} %get-tuple-element.6), kind=kOutput, calls=%fused_computation.24 | convolution fusion | flops 536870912 | bytes 5505024 | tf_op jit(solution)/shard_map/rop,odp->rd/dot_general | solution.py:105
  154.4 1.1 fusion.22
  155.6 0.7 pad_maximum_fusion
  156.4 0.6 copy.75
  (60 shorter events, 1.6 us)
Async XLA Ops:
  0.6 6.6 %collective-permute-start = (bf16[64,2,64,128]{3,2,1,0:T(8,128)(2,1)}, bf16[64,2,64,128]{3,2,1,0:T(8,128)(2,1)S(1)}, u32[]{:S(2)}, u32[]{:S(2)}) collective-permute-start(bf16[64,2,64,128]{3,2,1,0:T(8,128)(2,1)} %param.5), channel_id=1, source_target_pairs={{0,1},{1,0},{2,3},{3,2},{4,5},{5,4},{6,7},{7,6},{8,9},{9,8},{10,11... | collective-permute-start | bytes 6291464 | tf_op jit(solution)/shard_map/ppermute | solution.py:12
  17.7 13.1 %copy-start.6 = (bf16[2,2,64,128]{3,2,1,0:T(8,128)(2,1)S(1)}, bf16[2,2,64,128]{3,2,1,0:T(8,128)(2,1)}, u32[]{:S(2)}) copy-start(bf16[2,2,64,128]{3,2,1,0:T(8,128)(2,1)} %param.7) | copy-start | bytes 196612
  17.7 16.0 %copy-start.9 = (s32[64]{0:T(128)S(1)}, s32[64]{0:T(128)}, u32[]{:S(2)}) copy-start(s32[64]{0:T(128)} %param.9) | copy-start | bytes 772
  17.7 18.1 %copy-start.5 = (bf16[2,128,512]{2,1,0:T(8,128)(2,1)S(1)}, bf16[2,128,512]{2,1,0:T(8,128)(2,1)}, u32[]{:S(2)}) copy-start(bf16[2,128,512]{2,1,0:T(8,128)(2,1)} %param.6) | copy-start | bytes 786436
  17.7 113.5 %all-to-all-start = ((bf16[32,2,2,128,128]{4,3,2,1,0:T(8,128)(2,1)}), bf16[32,2,2,128,128]{4,3,2,1,0:T(8,128)(2,1)}, u32[]{:S(2)}, u32[]{:S(2)}) async-start(bf16[32,2,2,128,128]{4,3,2,1,0:T(8,128)(2,1)} %bitcast.115), calls=%async_computation | async-start | bytes 8388608 | tf_op jit(solution)/shard_map/all_to_all | solution.py:64
  30.8 6.9 %collective-permute-start.1 = (bf16[2,2,64,128]{3,2,1,0:T(8,128)(2,1)S(1)}, bf16[2,2,64,128]{3,2,1,0:T(8,128)(2,1)S(1)}, u32[]{:S(2)}, u32[]{:S(2)}) collective-permute-start(bf16[2,2,64,128]{3,2,1,0:T(8,128)(2,1)S(1)} %copy-done.6), channel_id=1, source_target_pairs={{0,1},{1,0},{2,3},{3,2},{4,5},{5,4},{6,7},{7,6},{8,9},{9,8},{10,11... | collective-permute-start | bytes 196616 | tf_op jit(solution)/shard_map/ppermute | solution.py:12
  37.7 0.7 copy-start.3
  38.7 92.5 %collective-permute-start.2 = (bf16[2,2,64,128]{3,2,1,0:T(8,128)(2,1)S(1)}, bf16[2,2,64,128]{3,2,1,0:T(8,128)(2,1)S(1)}, u32[]{:S(2)}, u32[]{:S(2)}) collective-permute-start(bf16[2,2,64,128]{3,2,1,0:T(8,128)(2,1)S(1)} %pad_maximum_fusion.3), channel_id=1, source_target_pairs={{0,256},{16,272},{32,288},{48,304},{64,320},{80,336},{96,352},{112... | collective-permute-start | bytes 196616 | tf_op jit(solution)/shard_map/ppermute | solution.py:17
  131.2 1.7 %copy-start.7 = (bf16[2,2,64,128]{3,2,1,0:T(8,128)(2,1)}, bf16[2,2,64,128]{3,2,1,0:T(8,128)(2,1)S(1)}, u32[]{:S(2)}) copy-start(bf16[2,2,64,128]{3,2,1,0:T(8,128)(2,1)S(1)} %collective-permute-done.2) | copy-start | bytes 196612
  134.3 1.3 copy-start.1
  135.6 1.3 copy-start
  135.6 1.3 copy-start.2
  147.8 2.5 %copy-start.4 = (bf16[2,2,128,128]{3,2,1,0:T(8,128)(2,1)S(1)}, bf16[2,2,128,128]{3,2,1,0:T(8,128)(2,1)}, u32[]{:S(2)}) copy-start(bf16[2,2,128,128]{3,2,1,0:T(8,128)(2,1)} %copy-done.3) | copy-start | bytes 393220
  150.6 5.7 %copy-start.8 = (bf16[2,2,64,128]{3,2,1,0:T(8,128)(2,1)S(1)}, bf16[2,2,64,128]{3,2,1,0:T(8,128)(2,1)}, u32[]{:S(2)}) copy-start(bf16[2,2,64,128]{3,2,1,0:T(8,128)(2,1)} %copy-done.7) | copy-start | bytes 196612
where the time goes:
time: 157 us
  waiting for transfers between devices  85.9 us (55%)
  starting transfers between devices  25.7 us (16%)
  other arithmetic  20.8 us (13%)
  matrix products  11.3 us (7%)
  local copies, waits for them, and re-layouts  10.8 us (7%)
  between operations  2.41 us (2%)
    ppermute x1, waiting for transfers between devices, from_behind(): lax.ppermute(array, axis, [(i, (i + by) % devices) for i in range(devices)])  82.7 us
    all_to_all x1, starting transfers between devices, on_device(): lax.all_to_all(outgoing, 'pool', split_axis=0, concat_axis=0, tiled=True)  13.1 us
    ppermute x1, starting transfers between devices, from_behind(): lax.ppermute(array, axis, [(i, (i + by) % devices) for i in range(devices)])  7.19 us
    dot_general x2, matrix products, on_device(): jnp.einsum('rop,odp->rd', page_part, arrived[:, request, 1], preferred_el...  6.27 us
    reduce_sum x1, other arithmetic, on_device(): totals = jnp.sum(weights, axis=1, keepdims=True)  6.11 us
    ppermute x2, starting transfers between devices, partner_2(): return lax.ppermute(value, axis, pairs)  5.43 us
    select_n x2, other arithmetic, joined(): jnp.where(lower_half, jnp.concatenate([mine, partner], axis=-2), jnp.conc...  5.3 us
    gather x1, local copies, waits for them, and re-layouts, on_device(): whole_pool[slot_of]  5.22 us
  transfers between devices with their start and end apart: 4, of which 2 were waited for; matrix products, arithmetic and copies ran while one was open for 4% of the time, Pallas kernels for 0%

commit v1 on v0

v1 whole, which is shorter than its diff:
```python
import functools
import math

import jax
import jax.numpy as jnp
from jax import lax
from jax.experimental import pallas as pl
from jax.experimental.pallas import tpu as pltpu
from jax.sharding import Mesh
from jax.sharding import PartitionSpec as P

MIB = 1024 * 1024
GROUP = ("pool", "core")


def swap_cores(array):
    return lax.ppermute(array, "core", [(0, 1), (1, 0)])


def from_behind(array, axis, by):
    devices = lax.axis_size(axis)
    return lax.ppermute(array, axis, [(i, (i + by) % devices) for i in range(devices)])


def angles_of(positions, head_width):
    indices = jnp.arange(head_width // 2, dtype=jnp.float32)
    inverse = jnp.power(jnp.float32(1000000.0), -2.0 * indices / head_width)
    return positions.astype(jnp.float32)[:, None] * inverse[None, :]


def pack_kernel(part, slots_ref, pool_ref, out_ref, sem):
    count = out_ref.shape[0]

    @pl.loop(0, count, unroll=8)
    def _(r):
        pltpu.make_async_copy(pool_ref.at[slots_ref[r], part], out_ref.at[r], sem).start()

    pltpu.make_async_copy(out_ref, out_ref, sem).wait()


def pack(part, slots, pool_kv):
    count = slots.shape[0]
    _, _, half, page = pool_kv.shape
    return pl.pallas_call(
        functools.partial(pack_kernel, part),
        grid_spec=pltpu.PrefetchScalarGridSpec(
            num_scalar_prefetch=1,
            grid=(1,),
            in_specs=[pl.BlockSpec(memory_space=pl.ANY)],
            out_specs=pl.BlockSpec(memory_space=pl.ANY),
            scratch_shapes=[pltpu.SemaphoreType.DMA],
        ),
        out_shape=jax.ShapeDtypeStruct((count, half, page), pool_kv.dtype),
        compiler_params=pltpu.CompilerParams(vmem_limit_bytes=2 * MIB),
        cost_estimate=pl.CostEstimate(
            flops=0, bytes_accessed=2 * count * half * page * 2, transcendentals=0
        ),
        name="pack_pages",
    )(slots, pool_kv)


def weigh_kernel(heads, live_ref, q_ref, cos_ref, sin_ref, keys_ref, fresh_ref,
                 w_ref, wf_ref, totals_ref, rq_ref, scores_ref, own_ref, peak_ref):
    tokens = q_ref.shape[1]
    width = cos_ref.shape[1]
    pairs = w_ref.shape[1]
    page = fresh_ref.shape[1]
    rows = heads * tokens
    scale = 1.0 / math.sqrt(width)
    for h in range(heads):
        x = q_ref[0, :, h * width:(h + 1) * width].astype(jnp.float32)
        turned = pltpu.roll(x, width // 2, 1)
        rq_ref[h * tokens:(h + 1) * tokens, :] = (
            x * cos_ref[...] + turned * sin_ref[...]
        ).astype(jnp.bfloat16)
    rq = rq_ref[...]
    own = jnp.dot(rq, fresh_ref[...], preferred_element_type=jnp.float32) * scale
    token = lax.rem(lax.broadcasted_iota(jnp.int32, (rows, page), 0), tokens)
    key = lax.broadcasted_iota(jnp.int32, (rows, page), 1)
    own = jnp.where(key <= token, own, -jnp.inf)
    own_ref[...] = own
    peak_ref[...] = own
    lane = lax.broadcasted_iota(jnp.int32, (1, 2 * page), 1)

    @pl.loop(0, pairs)
    def _(g):
        block = jnp.concatenate([keys_ref[2 * g], keys_ref[2 * g + 1]], axis=1)
        one = jnp.where(live_ref[2 * g] > 0, 0.0, -1e30)
        two = jnp.where(live_ref[2 * g + 1] > 0, 0.0, -1e30)
        bias = jnp.where(lane < page, one, two)
        s = jnp.dot(rq, block, preferred_element_type=jnp.float32) * scale + bias
        scores_ref[g] = s
        peak_ref[...] = jnp.maximum(
            peak_ref[...], jnp.maximum(s[:, :page], s[:, page:])
        )

    largest = jnp.max(peak_ref[...], axis=1, keepdims=True)
    w = jnp.exp(own_ref[...] - largest)
    wf_ref[0] = w.astype(jnp.bfloat16)
    own_ref[...] = w
    peak_ref[...] = jnp.broadcast_to(largest, (rows, page))

    @pl.loop(0, pairs)
    def _(g):
        top = peak_ref[...]
        a = jnp.exp(scores_ref[g, :, :page] - top)
        b = jnp.exp(scores_ref[g, :, page:] - top)
        w_ref[0, g, :, :page] = a.astype(jnp.bfloat16)
        w_ref[0, g, :, page:] = b.astype(jnp.bfloat16)
        own_ref[...] += a + b

    totals_ref[0] = jnp.broadcast_to(
        jnp.sum(own_ref[...], axis=1, keepdims=True), (rows, page)
    )


def weigh(live, q, cosine, sine, keys, fresh):
    sets, tokens, wide = q.shape
    pages, width, page = keys.shape
    heads = wide // width
    rows = heads * tokens
    pairs = pages // 2
    whole = lambda *shape: pl.BlockSpec(shape, lambda s, *_: (0,) * len(shape))
    each = lambda *shape: pl.BlockSpec((1,) + shape, lambda s, *_: (s,) + (0,) * len(shape))
    return pl.pallas_call(
        functools.partial(weigh_kernel, heads),
        grid_spec=pltpu.PrefetchScalarGridSpec(
            num_scalar_prefetch=1,
            grid=(sets,),
            in_specs=[
                each(tokens, wide),
                whole(tokens, width),
                whole(tokens, width),
                whole(pages, width, page),
                whole(width, page),
            ],
            out_specs=[
                each(pairs, rows, 2 * page),
                each(rows, page),
                each(rows, page),
            ],
            scratch_shapes=[
                pltpu.VMEM((rows, width), jnp.bfloat16),
                pltpu.VMEM((pairs, rows, 2 * page), jnp.float32),
                pltpu.VMEM((rows, page), jnp.float32),
                pltpu.VMEM((rows, page), jnp.float32),
            ],
        ),
        out_shape=[
            jax.ShapeDtypeStruct((sets, pairs, rows, 2 * page), jnp.bfloat16),
            jax.ShapeDtypeStruct((sets, rows, page), jnp.bfloat16),
            jax.ShapeDtypeStruct((sets, rows, page), jnp.float32),
        ],
        compiler_params=pltpu.CompilerParams(vmem_limit_bytes=32 * MIB),
        cost_estimate=pl.CostEstimate(
            flops=2 * sets * rows * pages * page * width,
            bytes_accessed=sets * rows * pages * page * 2,
            transcendentals=sets * rows * pages * page,
        ),
        name="weigh_keys",
    )(live, q, cosine, sine, keys, fresh)


def gather_kernel(heads, w_ref, wf_ref, totals_ref, values_ref, fresh_ref, out_ref, acc_ref):
    step = pl.program_id(0)
    tokens, wide = out_ref.shape
    width = wide // heads
    contract_last = (((1,), (1,)), ((), ()))

    @pl.when(step == 0)
    def _():
        acc_ref[...] = lax.dot_general(
            wf_ref[0], fresh_ref[...], contract_last, preferred_element_type=jnp.float32
        )

    total = acc_ref[...]
    for g in range(w_ref.shape[1]):
        block = jnp.concatenate([values_ref[2 * g], values_ref[2 * g + 1]], axis=1)
        total += lax.dot_general(
            w_ref[0, g], block, contract_last, preferred_element_type=jnp.float32
        )
    acc_ref[...] = total

    @pl.when(step == pl.num_programs(0) - 1)
    def _():
        done = (acc_ref[...] / totals_ref[0]).astype(jnp.bfloat16)
        for h in range(heads):
            out_ref[:, h * width:(h + 1) * width] = done[h * tokens:(h + 1) * tokens, :]


def attend(which, tokens, w, wf, totals, values, fresh):
    _, pairs, rows, two_pages = w.shape
    page = two_pages // 2
    width = fresh.shape[0]
    heads = rows // tokens
    steps = 4
    per = pairs // steps
    return pl.pallas_call(
        functools.partial(gather_kernel, heads),
        grid=(steps,),
        in_specs=[
            pl.BlockSpec((1, per, rows, two_pages), lambda s: (which, s, 0, 0)),
            pl.BlockSpec((1, rows, page), lambda s: (which, 0, 0)),
            pl.BlockSpec((1, rows, page), lambda s: (which, 0, 0)),
            pl.BlockSpec((2 * per, width, page), lambda s: (s, 0, 0)),
            pl.BlockSpec((width, page), lambda s: (0, 0)),
        ],
        out_specs=pl.BlockSpec((tokens, heads * width), lambda s: (0, 0)),
        scratch_shapes=[pltpu.VMEM((rows, width), jnp.float32)],
        out_shape=jax.ShapeDtypeStruct((tokens, heads * width), jnp.bfloat16),
        compiler_params=pltpu.CompilerParams(vmem_limit_bytes=12 * MIB),
        cost_estimate=pl.CostEstimate(
            flops=2 * rows * pairs * two_pages * width,
            bytes_accessed=rows * pairs * two_pages * 2,
            transcendentals=0,
        ),
        name="attend_values",
    )(w, wf, totals, values, fresh)


def on_device(pool_kv, queries, new_kv, page_table, prefix_pages):
    pool_count = lax.axis_size("pool")
    pool_rank = lax.axis_index("pool")
    core = lax.axis_index("core")
    lower_half = core == 0
    slot_count, _, half_width, page_len = pool_kv.shape
    head_width = 2 * half_width
    local_requests, suffix_len, _ = queries.shape
    owner_of = page_table // slot_count
    slot_of = jnp.sum(jnp.where(owner_of == pool_rank, page_table % slot_count, 0), axis=1)

    sent_keys = pack(0, slot_of, pool_kv)
    page_keys = lax.all_to_all(sent_keys, GROUP, split_axis=0, concat_axis=0, tiled=True)
    sent_values = pack(1, slot_of, pool_kv)
    page_values = lax.all_to_all(sent_values, GROUP, split_axis=0, concat_axis=0, tiled=True)
    page_keys = page_keys.reshape(pool_count, head_width, page_len)
    page_values = page_values.reshape(pool_count, head_width, page_len)

    first_row = pool_rank * local_requests
    own_owners = lax.dynamic_index_in_dim(owner_of, first_row + core, 0, keepdims=False)
    owner_ids = jnp.arange(pool_count, dtype=jnp.int32)
    live = jnp.any(own_owners[None, :] == owner_ids[:, None], axis=1).astype(jnp.int32)
    own_lengths = lax.dynamic_slice_in_dim(prefix_pages, first_row, local_requests, 0)

    given = lax.dynamic_index_in_dim(queries, 1 - core, 0, keepdims=False)
    kept = lax.dynamic_index_in_dim(queries, core, 0, keepdims=False)
    other_fresh = swap_cores(new_kv)
    taken = swap_cores(given)

    positions = own_lengths[:, None] * page_len + jnp.arange(suffix_len, dtype=jnp.int32)
    angles = angles_of(positions.reshape(-1), head_width).reshape(
        local_requests, suffix_len, half_width
    )
    cosine, sine = jnp.cos(angles), jnp.sin(angles)
    own_cosine = lax.dynamic_index_in_dim(cosine, core, 0, keepdims=False)
    own_sine = lax.dynamic_index_in_dim(sine, core, 0, keepdims=False)
    q_cosine = jnp.concatenate([own_cosine, own_cosine], axis=1)
    q_sine = jnp.concatenate([-own_sine, own_sine], axis=1)

    first = jnp.where(lower_half, new_kv[:, 0], other_fresh[:, 0]).astype(jnp.float32)
    second = jnp.where(lower_half, other_fresh[:, 0], new_kv[:, 0]).astype(jnp.float32)
    k_cosine = jnp.swapaxes(cosine, 1, 2)
    k_sine = jnp.swapaxes(sine, 1, 2)
    rotated_first = (first * k_cosine - second * k_sine).astype(jnp.bfloat16)
    rotated_second = (second * k_cosine + first * k_sine).astype(jnp.bfloat16)
    own_keys = jnp.where(lower_half, rotated_first, rotated_second)
    landing = jnp.stack([own_keys, new_kv[:, 1]], axis=1)
    landed = from_behind(landing, "pool", pool_count // 2)

    fresh_keys = lax.dynamic_index_in_dim(
        jnp.concatenate([rotated_first, rotated_second], axis=1), core, 0, keepdims=False
    )
    mine = lax.dynamic_index_in_dim(new_kv[:, 1], core, 0, keepdims=False)
    theirs = lax.dynamic_index_in_dim(other_fresh[:, 1], core, 0, keepdims=False)
    fresh_values = jnp.where(
        lower_half,
        jnp.concatenate([mine, theirs], axis=0),
        jnp.concatenate([theirs, mine], axis=0),
    )

    w, wf, totals = weigh(
        live, jnp.stack([taken, kept], axis=0), q_cosine, q_sine, page_keys, fresh_keys
    )
    for_partner = attend(0, suffix_len, w, wf, totals, page_values, fresh_values)
    from_partner = swap_cores(for_partner)
    stays = attend(1, suffix_len, w, wf, totals, page_values, fresh_values)
    attended = jnp.where(
        lower_half,
        jnp.stack([stays, from_partner], axis=0),
        jnp.stack([from_partner, stays], axis=0),
    )
    return (attended, landed)


def solution(mesh):
    pool_count, tp_count = mesh.devices.shape
    cores = Mesh(mesh.devices.reshape(pool_count, tp_count // 2, 2), ("pool", "head", "core"))
    tp = ("head", "core")
    return jax.shard_map(
        on_device,
        mesh=cores,
        in_specs=(
            P("pool", None, tp, None),
            P("pool", None, tp),
            P("pool", None, tp, None),
            P(),
            P(),
        ),
        out_specs=(P("pool", None, tp), P("pool", None, tp, None)),
        check_vma=False,
    )
```

time: 157 us -> 105 us (0.67)
  the two profiles are of different devices: /device:TPU:35 before, /device:TPU:1 now
where the time goes in v1:
time: 105 us; the launch traced here: 103 us
  waiting for transfers between devices  35 us (33%)
  starting transfers between devices  32.7 us (31%)
  Pallas kernels  19.2 us (18%)
  local copies, waits for them, and re-layouts  12.7 us (12%)
  other arithmetic  2.94 us (3%)
    all_to_all x1, waiting for transfers between devices, on_device(): lax.all_to_all(sent_keys, GROUP, split_axis=0, concat_axis=0, tiled=True)  18.3 us
    all_to_all x1, starting transfers between devices, on_device(): lax.all_to_all(sent_keys, GROUP, split_axis=0, concat_axis=0, tiled=True)  14.8 us
    pallas_call x1, Pallas kernels, weigh(): pl.pallas_call(functools.partial(weigh_kernel, heads), grid_spec=pltpu.Pr...  12 us
    unnamed x14, local copies, waits for them, and re-layouts  11.2 us
    all_to_all x1, waiting for transfers between devices, on_device(): lax.all_to_all(sent_values, GROUP, split_axis=0, concat_axis=0, tiled=True)  11 us
    ppermute x3, starting transfers between devices, swap_cores(): return lax.ppermute(array, 'core', [(0, 1), (1, 0)])  7.58 us
    all_to_all x1, starting transfers between devices, on_device(): lax.all_to_all(sent_values, GROUP, split_axis=0, concat_axis=0, tiled=True)  6.46 us
    ppermute x1, waiting for transfers between devices, from_behind(): lax.ppermute(array, axis, [(i, (i + by) % devices) for i in range(devices)])  5.72 us
  transfers between devices with their start and end apart: 6, of which 3 were waited for; matrix products, arithmetic and copies ran while one was open for 4% of the time, Pallas kernels for 15%

profile of v1, /device:TPU:1, one launch (start us, length us, event | category | flops | bytes accessed | tf_op | source)
XLA Modules:
  0.0 103.4 jit_solution(5061661641749512844)
XLA Ops:
  0.6 0.8 fusion.17
  1.4 1.6 %copy-done.2 = bf16[64,2,64,128]{3,2,1,0:T(8,128)(2,1)S(1)} copy-done((bf16[64,2,64,128]{3,2,1,0:T(8,128)(2,1)S(1)}, bf16[64,2,64,128]{3,2,1,0:T(8,128)(2,1)}, u32[]{:S(2)}) %copy-start.2) | copy-done | bytes 2097176
  3.0 1.5 %pack_pages.2 = bf16[64,64,128]{2,1,0:T(8,128)(2,1)} custom-call(s32[64]{0:T(128)S(1)} %get-tuple-element.17.slots_ref, bf16[64,2,64,128]{3,2,1,0:T(8,128)(2,1)S(1)} %copy-done.2), custom_call_target="tpu_custom_call" | custom-call | bytes 2097152 | tf_op jit(solution)/shard_map/pack_pages/pallas_call | solution.py:44
  4.5 14.8 %all-to-all-start = ((bf16[64,64,128]{2,1,0:T(8,128)(2,1)}), bf16[64,64,128]{2,1,0:T(8,128)(2,1)S(1)}, u32[]{:S(2)}, u32[]{:S(2)}) async-start(bf16[64,64,128]{2,1,0:T(8,128)(2,1)} %pack_pages.2), calls=%async_computation | async-start | bytes 2097152 | tf_op jit(solution)/shard_map/all_to_all | solution.py:233
  19.4 0.8 copy.19
  20.2 2.4 %collective-permute-start.1 = (bf16[2,2,64,128]{3,2,0,1:T(8,128)(2,1)S(1)}, bf16[2,2,64,128]{3,2,0,1:T(8,128)(2,1)S(1)}, u32[]{:S(2)}, u32[]{:S(2)}) collective-permute-start(bf16[2,2,64,128]{3,2,0,1:T(8,128)(2,1)S(1)} %copy.19), channel_id=1, source_target_pairs={{0,1},{1,0},{2,3},{3,2},{4,5},{5,4},{6,7},{7,6},{8,9},{9,8},{10,11... | collective-permute-start | bytes 196616 | tf_op jit(solution)/shard_map/ppermute | solution.py:17
  22.6 1.0 dynamic-slice_bitcast_fusion
  23.6 2.0 %collective-permute-start = (bf16[128,512]{1,0:T(8,128)(2,1)S(1)}, bf16[128,512]{1,0:T(8,128)(2,1)S(1)}, u32[]{:S(2)}, u32[]{:S(2)}) collective-permute-start(bf16[128,512]{1,0:T(8,128)(2,1)S(1)} %get-tuple-element.13), channel_id=1, source_target_pairs={{0,1},{1,0},{2,3},{3,2},{4,5},{5,4},{6,7},{7,6},{8,9},{9,8},{10,11... | collective-permute-start | bytes 393224 | tf_op jit(solution)/shard_map/ppermute | solution.py:17
  25.6 1.6 %copy-done.3 = bf16[64,2,64,128]{3,2,1,0:T(8,128)(2,1)S(1)} copy-done((bf16[64,2,64,128]{3,2,1,0:T(8,128)(2,1)S(1)}, bf16[64,2,64,128]{3,2,1,0:T(8,128)(2,1)}, u32[]{:S(2)}) %copy-start.3) | copy-done | bytes 2097176
  27.1 1.6 %pack_pages.3 = bf16[64,64,128]{2,1,0:T(8,128)(2,1)} custom-call(s32[64]{0:T(128)S(1)} %get-tuple-element.17.slots_ref, bf16[64,2,64,128]{3,2,1,0:T(8,128)(2,1)S(1)} %copy-done.3), custom_call_target="tpu_custom_call" | custom-call | bytes 2097152 | tf_op jit(solution)/shard_map/pack_pages/pallas_call | solution.py:44
  28.8 0.2 dynamic-slice_reduce_fusion
  28.9 0.1 fusion.19
  29.1 18.3 %all-to-all-done = bf16[64,64,128]{2,1,0:T(8,128)(2,1)S(1)} async-done(((bf16[64,64,128]{2,1,0:T(8,128)(2,1)}), bf16[64,64,128]{2,1,0:T(8,128)(2,1)S(1)}, u32[]{:S(2)}, u32[]{:S(2)}) %all-to-all-start) | async-done | bytes 1048608 | tf_op jit(solution)/shard_map/all_to_all | solution.py:233
  47.4 6.5 %all-to-all-start.1 = ((bf16[64,64,128]{2,1,0:T(8,128)(2,1)}), bf16[64,64,128]{2,1,0:T(8,128)(2,1)S(1)}, u32[]{:S(2)}, u32[]{:S(2)}) async-start(bf16[64,64,128]{2,1,0:T(8,128)(2,1)} %pack_pages.3), calls=%async_computation.1 | async-start | bytes 2097152 | tf_op jit(solution)/shard_map/all_to_all | solution.py:235
  53.9 0.1 dynamic-slice_multiply_fusion
  54.1 0.1 broadcast_multiply_fusion
  54.2 0.2 cosine_bitcast_fusion
  54.4 0.2 fusion.21
  54.6 0.1 pad_maximum_fusion.1
  54.8 0.3 bitcast_select_fusion
  55.1 0.3 fusion.13
  55.6 12.0 %weigh_keys.1 = (bf16[2,16,512,256]{3,2,1,0:T(8,128)(2,1)S(1)}, bf16[2,512,128]{2,1,0:T(8,128)(2,1)S(1)}, f32[2,512,128]{2,1,0:T(8,128)S(1)}) custom-call(s32[32]{0:T(128)S(1)} %convert_element_type.40.live_ref, bf16[2,128,512]{2,1,0:T(8,128)(2,1)S(1)} %pad_maximum_fusion.q_ref, f32[128,128]{1,0:T(8,128)S(1)} %get-tuple-element.19.cos_ref, ...), custom_call_target="tpu_custom_call" | custom-call | flops 1073741824 | bytes 8388608 | tf_op jit(solution)/shard_map/weigh_keys/pallas_call | solution.py:125
  67.6 3.2 %copy-done = bf16[2,16,512,256]{3,2,1,0:T(8,128)(2,1)} copy-done((bf16[2,16,512,256]{3,2,1,0:T(8,128)(2,1)}, bf16[2,16,512,256]{3,2,1,0:T(8,128)(2,1)S(1)}, u32[]{:S(2)}) %copy-start) | copy-done | bytes 8388632
  70.8 11.0 %all-to-all-done.1 = bf16[64,64,128]{2,1,0:T(8,128)(2,1)S(1)} async-done(((bf16[64,64,128]{2,1,0:T(8,128)(2,1)}), bf16[64,64,128]{2,1,0:T(8,128)(2,1)S(1)}, u32[]{:S(2)}, u32[]{:S(2)}) %all-to-all-start.1) | async-done | bytes 1048608 | tf_op jit(solution)/shard_map/all_to_all | solution.py:235
  81.8 3.4 %copy-done.1 = bf16[2,16,512,256]{3,2,1,0:T(8,128)(2,1)S(1)} copy-done((bf16[2,16,512,256]{3,2,1,0:T(8,128)(2,1)S(1)}, bf16[2,16,512,256]{3,2,1,0:T(8,128)(2,1)}, u32[]{:S(2)}) %copy-start.1) | copy-done | bytes 8388632
  85.2 2.0 %attend_values.3 = bf16[128,512]{1,0:T(8,128)(2,1)S(1)} custom-call(bf16[2,16,512,256]{3,2,1,0:T(8,128)(2,1)S(1)} %copy-done.1, bf16[2,512,128]{2,1,0:T(8,128)(2,1)S(1)} %get-tuple-element.6.wf_ref, f32[2,512,128]{2,1,0:T(8,128)S(1)} %get-tuple-element.7.totals_ref, bf16[32,128,128]{2,1,0:T(8,128)(2,1)S(1)} %bitcast.66, ...), custom_call_target="tpu_custom_call" | custom-call | flops 536870912 | bytes 4194304 | tf_op jit(solution)/shard_map/attend_values/pallas_call | solution.py:198
  87.2 3.3 %collective-permute-start.2 = (bf16[128,512]{1,0:T(8,128)(2,1)S(1)}, bf16[128,512]{1,0:T(8,128)(2,1)S(1)}, u32[]{:S(2)}, u32[]{:S(2)}) collective-permute-start(bf16[128,512]{1,0:T(8,128)(2,1)S(1)} %attend_values.3), channel_id=1, source_target_pairs={{0,1},{1,0},{2,3},{3,2},{4,5},{5,4},{6,7},{7,6},{8,9},{9,8},{10,11... | collective-permute-start | bytes 393224 | tf_op jit(solution)/shard_map/ppermute | solution.py:17
  90.5 3.8 %collective-permute-start.3 = (bf16[2,2,64,128]{3,2,1,0:T(8,128)(2,1)S(1)}, bf16[2,2,64,128]{3,2,1,0:T(8,128)(2,1)S(1)}, u32[]{:S(2)}, u32[]{:S(2)}) collective-permute-start(bf16[2,2,64,128]{3,2,1,0:T(8,128)(2,1)S(1)} %pad_maximum_fusion.3), channel_id=1, source_target_pairs={{0,256},{16,272},{32,288},{48,304},{64,320},{80,336},{96,352},{112... | collective-permute-start | bytes 196616 | tf_op jit(solution)/shard_map/ppermute | solution.py:22
  94.3 5.7 %collective-permute-done.3 = bf16[2,2,64,128]{3,2,1,0:T(8,128)(2,1)S(1)} collective-permute-done((bf16[2,2,64,128]{3,2,1,0:T(8,128)(2,1)S(1)}, bf16[2,2,64,128]{3,2,1,0:T(8,128)(2,1)S(1)}, u32[]{:S(2)}, u32[]{:S(2)}) %collective-permute-start.3) | collective-permute-done | bytes 65568 | tf_op jit(solution)/shard_map/ppermute | solution.py:22
  100.0 2.0 %attend_values.2 = bf16[128,512]{1,0:T(8,128)(2,1)S(1)} custom-call(bf16[2,16,512,256]{3,2,1,0:T(8,128)(2,1)S(1)} %copy-done.1, bf16[2,512,128]{2,1,0:T(8,128)(2,1)S(1)} %get-tuple-element.6.wf_ref, f32[2,512,128]{2,1,0:T(8,128)S(1)} %get-tuple-element.7.totals_ref, bf16[32,128,128]{2,1,0:T(8,128)(2,1)S(1)} %bitcast.67, ...), custom_call_target="tpu_custom_call" | custom-call | flops 536870912 | bytes 4194304 | tf_op jit(solution)/shard_map/attend_values/pallas_call | solution.py:198
  102.0 0.7 maximum_select_fusion
  102.8 0.6 copy.28
  (22 shorter events, 0.2 us)
Async XLA Ops:
  0.6 53.3 %copy-start.5 = (s32[64]{0:T(128)S(1)}, s32[64]{0:T(128)}, u32[]{:S(2)}) copy-start(s32[64]{0:T(128)} %param.9) | copy-start | bytes 772
  1.4 1.6 %copy-start.2 = (bf16[64,2,64,128]{3,2,1,0:T(8,128)(2,1)S(1)}, bf16[64,2,64,128]{3,2,1,0:T(8,128)(2,1)}, u32[]{:S(2)}) copy-start(bf16[64,2,64,128]{3,2,1,0:T(8,128)(2,1)} %pool_ref.3) | copy-start | bytes 6291460
  3.0 50.9 %copy-start.4 = (bf16[2,2,64,128]{3,2,1,0:T(8,128)(2,1)S(1)}, bf16[2,2,64,128]{3,2,1,0:T(8,128)(2,1)}, u32[]{:S(2)}) copy-start(bf16[2,2,64,128]{3,2,1,0:T(8,128)(2,1)} %param.7) | copy-start | bytes 196612
  4.5 42.8 %all-to-all-start = ((bf16[64,64,128]{2,1,0:T(8,128)(2,1)}), bf16[64,64,128]{2,1,0:T(8,128)(2,1)S(1)}, u32[]{:S(2)}, u32[]{:S(2)}) async-start(bf16[64,64,128]{2,1,0:T(8,128)(2,1)} %pack_pages.2), calls=%async_computation | async-start | bytes 2097152 | tf_op jit(solution)/shard_map/all_to_all | solution.py:233
  20.2 34.5 %collective-permute-start.1 = (bf16[2,2,64,128]{3,2,0,1:T(8,128)(2,1)S(1)}, bf16[2,2,64,128]{3,2,0,1:T(8,128)(2,1)S(1)}, u32[]{:S(2)}, u32[]{:S(2)}) collective-permute-start(bf16[2,2,64,128]{3,2,0,1:T(8,128)(2,1)S(1)} %copy.19), channel_id=1, source_target_pairs={{0,1},{1,0},{2,3},{3,2},{4,5},{5,4},{6,7},{7,6},{8,9},{9,8},{10,11... | collective-permute-start | bytes 196616 | tf_op jit(solution)/shard_map/ppermute | solution.py:17
  23.6 31.9 %collective-permute-start = (bf16[128,512]{1,0:T(8,128)(2,1)S(1)}, bf16[128,512]{1,0:T(8,128)(2,1)S(1)}, u32[]{:S(2)}, u32[]{:S(2)}) collective-permute-start(bf16[128,512]{1,0:T(8,128)(2,1)S(1)} %get-tuple-element.13), channel_id=1, source_target_pairs={{0,1},{1,0},{2,3},{3,2},{4,5},{5,4},{6,7},{7,6},{8,9},{9,8},{10,11... | collective-permute-start | bytes 393224 | tf_op jit(solution)/shard_map/ppermute | solution.py:17
  25.6 1.6 %copy-start.3 = (bf16[64,2,64,128]{3,2,1,0:T(8,128)(2,1)S(1)}, bf16[64,2,64,128]{3,2,1,0:T(8,128)(2,1)}, u32[]{:S(2)}) copy-start(bf16[64,2,64,128]{3,2,1,0:T(8,128)(2,1)} %pool_ref.3) | copy-start | bytes 6291460
  47.4 34.5 %all-to-all-start.1 = ((bf16[64,64,128]{2,1,0:T(8,128)(2,1)}), bf16[64,64,128]{2,1,0:T(8,128)(2,1)S(1)}, u32[]{:S(2)}, u32[]{:S(2)}) async-start(bf16[64,64,128]{2,1,0:T(8,128)(2,1)} %pack_pages.3), calls=%async_computation.1 | async-start | bytes 2097152 | tf_op jit(solution)/shard_map/all_to_all | solution.py:235
  67.6 3.2 %copy-start = (bf16[2,16,512,256]{3,2,1,0:T(8,128)(2,1)}, bf16[2,16,512,256]{3,2,1,0:T(8,128)(2,1)S(1)}, u32[]{:S(2)}) copy-start(bf16[2,16,512,256]{3,2,1,0:T(8,128)(2,1)S(1)} %get-tuple-element.5.w_ref) | copy-start | bytes 25165828
  81.8 3.4 %copy-start.1 = (bf16[2,16,512,256]{3,2,1,0:T(8,128)(2,1)S(1)}, bf16[2,16,512,256]{3,2,1,0:T(8,128)(2,1)}, u32[]{:S(2)}) copy-start(bf16[2,16,512,256]{3,2,1,0:T(8,128)(2,1)} %copy-done) | copy-start | bytes 25165828
  87.2 14.8 %collective-permute-start.2 = (bf16[128,512]{1,0:T(8,128)(2,1)S(1)}, bf16[128,512]{1,0:T(8,128)(2,1)S(1)}, u32[]{:S(2)}, u32[]{:S(2)}) collective-permute-start(bf16[128,512]{1,0:T(8,128)(2,1)S(1)} %attend_values.3), channel_id=1, source_target_pairs={{0,1},{1,0},{2,3},{3,2},{4,5},{5,4},{6,7},{7,6},{8,9},{9,8},{10,11... | collective-permute-start | bytes 393224 | tf_op jit(solution)/shard_map/ppermute | solution.py:17
  90.5 9.5 %collective-permute-start.3 = (bf16[2,2,64,128]{3,2,1,0:T(8,128)(2,1)S(1)}, bf16[2,2,64,128]{3,2,1,0:T(8,128)(2,1)S(1)}, u32[]{:S(2)}, u32[]{:S(2)}) collective-permute-start(bf16[2,2,64,128]{3,2,1,0:T(8,128)(2,1)S(1)} %pad_maximum_fusion.3), channel_id=1, source_target_pairs={{0,256},{16,272},{32,288},{48,304},{64,320},{80,336},{96,352},{112... | collective-permute-start | bytes 196616 | tf_op jit(solution)/shard_map/ppermute | solution.py:22

commit v2 on v1

v2 whole, which is shorter than its diff:
```python
import functools
import math

import jax
import jax.numpy as jnp
from jax import lax
from jax.experimental import pallas as pl
from jax.experimental.pallas import tpu as pltpu
from jax.sharding import Mesh
from jax.sharding import PartitionSpec as P

MIB = 1024 * 1024
GROUP = ("pool", "core")
CONTRACT_LAST = (((1,), (1,)), ((), ()))
GROUPED = 4
STEPS = 4


def factor_of(width):
    return math.log2(math.e) / math.sqrt(width)


def swap_cores(array):
    return lax.ppermute(array, "core", [(0, 1), (1, 0)])


def from_behind(array, axis, by):
    devices = lax.axis_size(axis)
    return lax.ppermute(array, axis, [(i, (i + by) % devices) for i in range(devices)])


def angles_of(positions, head_width):
    indices = jnp.arange(head_width // 2, dtype=jnp.float32)
    inverse = jnp.power(jnp.float32(1000000.0), -2.0 * indices / head_width)
    return positions.astype(jnp.float32)[:, None] * inverse[None, :]


def pack_kernel(slots_ref, pool_ref, out_ref, sem):
    count = out_ref.shape[0]

    @pl.loop(0, count, unroll=8)
    def _(r):
        pltpu.make_async_copy(pool_ref.at[slots_ref[r]], out_ref.at[r], sem).start()

    pltpu.make_async_copy(out_ref, out_ref, sem).wait()


def pack(slots, pool_kv):
    shape = (slots.shape[0],) + pool_kv.shape[1:]
    return pl.pallas_call(
        pack_kernel,
        grid_spec=pltpu.PrefetchScalarGridSpec(
            num_scalar_prefetch=1,
            grid=(1,),
            in_specs=[pl.BlockSpec(memory_space=pl.ANY)],
            out_specs=pl.BlockSpec(memory_space=pl.ANY),
            scratch_shapes=[pltpu.SemaphoreType.DMA],
        ),
        out_shape=jax.ShapeDtypeStruct(shape, pool_kv.dtype),
        compiler_params=pltpu.CompilerParams(vmem_limit_bytes=2 * MIB),
        cost_estimate=pl.CostEstimate(
            flops=0, bytes_accessed=4 * math.prod(shape), transcendentals=0
        ),
        name="pack_pages",
    )(slots, pool_kv)


def own_scores(rq, fresh_keys, tokens):
    rows, page = rq.shape[0], fresh_keys.shape[1]
    own = jnp.dot(rq, fresh_keys, preferred_element_type=jnp.float32)
    token = lax.rem(lax.broadcasted_iota(jnp.int32, (rows, page), 0), tokens)
    key = lax.broadcasted_iota(jnp.int32, (rows, page), 1)
    return jnp.where(key <= token, own, -1e30)


def prepare_kernel(heads, factor, q_ref, cos_ref, sin_ref, keys_ref, values_ref,
                   rq_ref, state_ref):
    tokens = q_ref.shape[1]
    width = cos_ref.shape[1]
    rows = heads * tokens
    parts = []
    for h in range(heads):
        x = q_ref[0, :, h * width:(h + 1) * width].astype(jnp.float32)
        turned = pltpu.roll(x, width // 2, 1)
        parts.append((x * cos_ref[...] + turned * sin_ref[...]).astype(jnp.bfloat16))
    rq = jnp.concatenate(parts, axis=0)
    own = own_scores(rq, keys_ref[...], tokens)
    shift = jnp.max(own, axis=1, keepdims=True).astype(jnp.bfloat16).astype(jnp.float32)
    lane = lax.broadcasted_iota(jnp.int32, (rows, width), 1)
    extra = jnp.where(lane == 0, -shift, jnp.where(lane == 1, 1.0, 0.0))
    rq_ref[0, :, :width] = rq
    rq_ref[0, :, width:] = extra.astype(jnp.bfloat16)
    w = jnp.exp2((own - shift) * factor)
    state_ref[0, :, :width] = lax.dot_general(
        w.astype(jnp.bfloat16), values_ref[...], CONTRACT_LAST,
        preferred_element_type=jnp.float32,
    )
    state_ref[0, :, width:] = jnp.broadcast_to(jnp.sum(w, axis=1, keepdims=True), (rows, width))


def prepare(q, cosine, sine, fresh_keys, fresh_values):
    sets, tokens, wide = q.shape
    width, page = fresh_keys.shape
    heads = wide // width
    rows = heads * tokens
    whole = lambda *shape: pl.BlockSpec(shape, lambda s: (0,) * len(shape))
    each = lambda *shape: pl.BlockSpec((1,) + shape, lambda s: (s,) + (0,) * len(shape))
    return pl.pallas_call(
        functools.partial(prepare_kernel, heads, factor_of(width)),
        grid=(sets,),
        in_specs=[
            each(tokens, wide),
            whole(tokens, width),
            whole(tokens, width),
            whole(width, page),
            whole(width, page),
        ],
        out_specs=[each(rows, 2 * width), each(rows, 2 * width)],
        out_shape=[
            jax.ShapeDtypeStruct((sets, rows, 2 * width), jnp.bfloat16),
            jax.ShapeDtypeStruct((sets, rows, 2 * width), jnp.float32),
        ],
        compiler_params=pltpu.CompilerParams(vmem_limit_bytes=16 * MIB),
        cost_estimate=pl.CostEstimate(
            flops=4 * sets * rows * page * width,
            bytes_accessed=sets * rows * 2 * width * 6,
            transcendentals=sets * rows * page,
        ),
        name="prepare_queries",
    )(q, cosine, sine, fresh_keys, fresh_values)


def attend_kernel(heads, factor, live_ref, rq_ref, state_ref, kv_ref, keys_ref, values_ref,
                  all_ref, out_ref, acc_ref, page_ref, top_ref, sem):
    step = pl.program_id(0)
    tokens, wide = out_ref.shape
    width = wide // heads
    rows = heads * tokens
    page = kv_ref.shape[4]
    count = kv_ref.shape[0]
    first = step * count

    @pl.when(step == 0)
    def _():
        acc_ref[...] = state_ref[0]

    row = lax.broadcasted_iota(jnp.int32, (width, page), 0)

    def flags(p):
        hidden = jnp.where(live_ref[p] > 0, 0.0, -1e30)
        return jnp.where(row == 0, 1.0, jnp.where(row == 1, hidden, 0.0)).astype(jnp.bfloat16)

    ones = jnp.ones((width, GROUPED * page), jnp.bfloat16)
    rq = rq_ref[0]
    for at in range(0, count, GROUPED):
        weights, values = [], []
        for p in range(at, at + GROUPED, 2):
            keys = jnp.concatenate(
                [
                    jnp.concatenate(
                        [kv_ref[p + i, 0, 0], kv_ref[p + i, 1, 0], flags(first + p + i)], axis=0
                    )
                    for i in range(2)
                ],
                axis=1,
            )
            s = jnp.dot(rq, keys, preferred_element_type=jnp.float32)
            weights.append(jnp.exp2(s * factor).astype(jnp.bfloat16))
        for p in range(at, at + GROUPED):
            values.append(jnp.concatenate([kv_ref[p, 0, 1], kv_ref[p, 1, 1]], axis=0))
        block = jnp.concatenate([jnp.concatenate(values, axis=1), ones], axis=0)
        acc_ref[...] += lax.dot_general(
            jnp.concatenate(weights, axis=1), block, CONTRACT_LAST,
            preferred_element_type=jnp.float32,
        )

    @pl.when(step == pl.num_programs(0) - 1)
    def _():
        largest_total = jnp.max(acc_ref[:, width:])

        @pl.when(jnp.logical_not(largest_total <= 1e30))
        def _():
            exact(factor, tokens, width, live_ref, rq_ref, keys_ref, values_ref, all_ref,
                  acc_ref, page_ref, top_ref, sem)

        done = (acc_ref[:, :width] / acc_ref[:, width:]).astype(jnp.bfloat16)
        for h in range(heads):
            out_ref[:, h * width:(h + 1) * width] = done[h * tokens:(h + 1) * tokens, :]


def exact(factor, tokens, width, live_ref, rq_ref, keys_ref, values_ref, all_ref,
          acc_ref, page_ref, top_ref, sem):
    rows = rq_ref.shape[1]
    pages = all_ref.shape[0]
    half = width // 2
    rq = rq_ref[0, :, :width]
    own = own_scores(rq, keys_ref[...], tokens)
    top_ref[...] = own

    def scores_of(p):
        copy = pltpu.make_async_copy(all_ref.at[p], page_ref, sem)
        copy.start()
        copy.wait()
        keys = jnp.concatenate([page_ref[0, 0], page_ref[1, 0]], axis=0)
        hidden = jnp.where(live_ref[p] > 0, 0.0, -1e30)
        return jnp.dot(rq, keys, preferred_element_type=jnp.float32) + hidden

    @pl.loop(0, pages)
    def _(p):
        top_ref[...] = jnp.maximum(top_ref[...], scores_of(p))

    top_ref[...] = jnp.broadcast_to(
        jnp.max(top_ref[...], axis=1, keepdims=True), top_ref.shape
    )
    w = jnp.exp2((own - top_ref[...]) * factor)
    acc_ref[:, :width] = lax.dot_general(
        w.astype(jnp.bfloat16), values_ref[...], CONTRACT_LAST,
        preferred_element_type=jnp.float32,
    )
    acc_ref[:, width:] = jnp.broadcast_to(jnp.sum(w, axis=1, keepdims=True), (rows, width))

    @pl.loop(0, pages)
    def _(p):
        w = jnp.exp2((scores_of(p) - top_ref[...]) * factor)
        values = jnp.concatenate([page_ref[0, 1], page_ref[1, 1]], axis=0)
        acc_ref[:, :width] += lax.dot_general(
            w.astype(jnp.bfloat16), values, CONTRACT_LAST, preferred_element_type=jnp.float32
        )
        acc_ref[:, width:] += jnp.broadcast_to(
            jnp.sum(w, axis=1, keepdims=True), (rows, width)
        )


def attend(which, tokens, live, rq, state, arrived, fresh_keys, fresh_values):
    _, rows, double = rq.shape
    pages, _, _, half, page = arrived.shape
    width = double // 2
    heads = rows // tokens
    steps = STEPS
    per = pages // steps
    return pl.pallas_call(
        functools.partial(attend_kernel, heads, factor_of(width)),
        grid_spec=pltpu.PrefetchScalarGridSpec(
            num_scalar_prefetch=1,
            grid=(steps,),
            in_specs=[
                pl.BlockSpec((1, rows, double), lambda s, *_: (which, 0, 0)),
                pl.BlockSpec((1, rows, double), lambda s, *_: (which, 0, 0)),
                pl.BlockSpec((per, 2, 2, half, page), lambda s, *_: (s, 0, 0, 0, 0)),
                pl.BlockSpec((width, page), lambda s, *_: (0, 0)),
                pl.BlockSpec((width, page), lambda s, *_: (0, 0)),
                pl.BlockSpec(memory_space=pl.ANY),
            ],
            out_specs=pl.BlockSpec((tokens, heads * width), lambda s, *_: (0, 0)),
            scratch_shapes=[
                pltpu.VMEM((rows, double), jnp.float32),
                pltpu.VMEM((2, 2, half, page), jnp.bfloat16),
                pltpu.VMEM((rows, page), jnp.float32),
                pltpu.SemaphoreType.DMA,
            ],
        ),
        out_shape=jax.ShapeDtypeStruct((tokens, heads * width), jnp.bfloat16),
        compiler_params=pltpu.CompilerParams(vmem_limit_bytes=40 * MIB),
        cost_estimate=pl.CostEstimate(
            flops=4 * rows * pages * page * width,
            bytes_accessed=pages * width * page * 4,
            transcendentals=rows * pages * page,
        ),
        name="attend_pages",
    )(live, rq, state, arrived, fresh_keys, fresh_values, arrived)


def on_device(pool_kv, queries, new_kv, page_table, prefix_pages):
    pool_count = lax.axis_size("pool")
    pool_rank = lax.axis_index("pool")
    core = lax.axis_index("core")
    lower_half = core == 0
    slot_count, _, half_width, page_len = pool_kv.shape
    head_width = 2 * half_width
    local_requests, suffix_len, _ = queries.shape
    owner_of = page_table // slot_count
    slot_of = jnp.sum(jnp.where(owner_of == pool_rank, page_table % slot_count, 0), axis=1)

    arrived = lax.all_to_all(
        pack(slot_of, pool_kv), GROUP, split_axis=0, concat_axis=0, tiled=True
    ).reshape(pool_count, 2, 2, half_width, page_len)

    first_row = pool_rank * local_requests
    own_owners = lax.dynamic_index_in_dim(owner_of, first_row + core, 0, keepdims=False)
    owner_ids = jnp.arange(pool_count, dtype=jnp.int32)
    live = jnp.any(own_owners[None, :] == owner_ids[:, None], axis=1).astype(jnp.int32)
    own_lengths = lax.dynamic_slice_in_dim(prefix_pages, first_row, local_requests, 0)

    given = lax.dynamic_index_in_dim(queries, 1 - core, 0, keepdims=False)
    kept = lax.dynamic_index_in_dim(queries, core, 0, keepdims=False)
    other_fresh = swap_cores(new_kv)
    taken = swap_cores(given)

    positions = own_lengths[:, None] * page_len + jnp.arange(suffix_len, dtype=jnp.int32)
    angles = angles_of(positions.reshape(-1), head_width).reshape(
        local_requests, suffix_len, half_width
    )
    cosine, sine = jnp.cos(angles), jnp.sin(angles)
    own_cosine = lax.dynamic_index_in_dim(cosine, core, 0, keepdims=False)
    own_sine = lax.dynamic_index_in_dim(sine, core, 0, keepdims=False)
    q_cosine = jnp.concatenate([own_cosine, own_cosine], axis=1)
    q_sine = jnp.concatenate([-own_sine, own_sine], axis=1)

    first = jnp.where(lower_half, new_kv[:, 0], other_fresh[:, 0]).astype(jnp.float32)
    second = jnp.where(lower_half, other_fresh[:, 0], new_kv[:, 0]).astype(jnp.float32)
    k_cosine = jnp.swapaxes(cosine, 1, 2)
    k_sine = jnp.swapaxes(sine, 1, 2)
    rotated_first = (first * k_cosine - second * k_sine).astype(jnp.bfloat16)
    rotated_second = (second * k_cosine + first * k_sine).astype(jnp.bfloat16)
    own_keys = jnp.where(lower_half, rotated_first, rotated_second)
    landing = jnp.stack([own_keys, new_kv[:, 1]], axis=1)
    landed = from_behind(landing, "pool", pool_count // 2)

    fresh_keys = lax.dynamic_index_in_dim(
        jnp.concatenate([rotated_first, rotated_second], axis=1), core, 0, keepdims=False
    )
    mine = lax.dynamic_index_in_dim(new_kv[:, 1], core, 0, keepdims=False)
    theirs = lax.dynamic_index_in_dim(other_fresh[:, 1], core, 0, keepdims=False)
    fresh_values = jnp.where(
        lower_half,
        jnp.concatenate([mine, theirs], axis=0),
        jnp.concatenate([theirs, mine], axis=0),
    )

    rq, state = prepare(
        jnp.stack([taken, kept], axis=0), q_cosine, q_sine, fresh_keys, fresh_values
    )
    arrived, landed = lax.optimization_barrier((arrived, landed))
    inputs = (live, rq, state, arrived, fresh_keys, fresh_values)
    for_partner = attend(0, suffix_len, *inputs)
    from_partner = swap_cores(for_partner)
    stays = attend(1, suffix_len, *inputs)
    attended = jnp.where(
        lower_half,
        jnp.stack([stays, from_partner], axis=0),
        jnp.stack([from_partner, stays], axis=0),
    )
    return (attended, landed)


def solution(mesh):
    pool_count, tp_count = mesh.devices.shape
    cores = Mesh(mesh.devices.reshape(pool_count, tp_count // 2, 2), ("pool", "head", "core"))
    tp = ("head", "core")
    return jax.shard_map(
        on_device,
        mesh=cores,
        in_specs=(
            P("pool", None, tp, None),
            P("pool", None, tp),
            P("pool", None, tp, None),
            P(),
            P(),
        ),
        out_specs=(P("pool", None, tp), P("pool", None, tp, None)),
        check_vma=False,
    )
```

time: 105 us -> 90.5 us (0.86); the launches traced: 103 us -> 90.1 us
  local copies, waits for them, and re-layouts: 12.7 us -> 5.85 us
  Pallas kernels: 19.2 us -> 12.8 us
  starting transfers between devices: 32.7 us -> 31.4 us
  waiting for transfers between devices: 35 us -> 36.2 us
    ppermute x1, waiting for transfers between devices: 5.72 us -> 36.2 us  [from_behind(): lax.ppermute(array, axis, [(i, (i + by) % devices) for i in range(devices)])]
    all_to_all x2 -> x1, waiting for transfers between devices: 29.3 us -> 0.01 us  [on_device(): lax.all_to_all(pack(slot_of, pool_kv), GROUP, split_axis=0, concat_axis=0...]
    pallas_call x5 -> x4, Pallas kernels: 19.2 us -> 12.8 us  [the longest x2 8.24 us: attend(): pl.pallas_call(functools.partial(attend_kernel, heads, factor_of(width)),...]
    all_to_all x2 -> x1, starting transfers between devices: 21.3 us -> 15 us  [on_device(): lax.all_to_all(pack(slot_of, pool_kv), GROUP, split_axis=0, concat_axis=0...]
    unnamed x14 -> x16, local copies, waits for them, and re-layouts: 11.2 us -> 5.38 us
    ppermute x1, starting transfers between devices: 3.78 us -> 7.3 us  [from_behind(): lax.ppermute(array, axis, [(i, (i + by) % devices) for i in range(devices)])]
    ppermute x3, starting transfers between devices: 7.58 us -> 9.1 us  [swap_cores(): return lax.ppermute(array, 'core', [(0, 1), (1, 0)])]
  transfers between devices with their start and end apart: 6 -> 5, of which waited for: 3 -> 1; matrix products, arithmetic and copies ran while one was open for 4% -> 2% of each run, Pallas kernels for 15% -> 6%
where the time goes in v2:
time: 90.5 us; the launch traced here: 90.1 us
  waiting for transfers between devices  36.2 us (40%)
  starting transfers between devices  31.4 us (35%)
  Pallas kernels  12.8 us (14%)
  local copies, waits for them, and re-layouts  5.85 us (6%)
  other arithmetic  2.93 us (3%)
  between operations  0.92 us (1%)
    ppermute x1, waiting for transfers between devices, from_behind(): lax.ppermute(array, axis, [(i, (i + by) % devices) for i in range(devices)])  36.2 us
    all_to_all x1, starting transfers between devices, on_device(): lax.all_to_all(pack(slot_of, pool_kv), GROUP, split_axis=0, concat_axis=0...  15 us
    ppermute x3, starting transfers between devices, swap_cores(): return lax.ppermute(array, 'core', [(0, 1), (1, 0)])  9.1 us
    pallas_call x2, Pallas kernels, attend(): pl.pallas_call(functools.partial(attend_kernel, heads, factor_of(width)),...  8.24 us
    ppermute x1, starting transfers between devices, from_behind(): lax.ppermute(array, axis, [(i, (i + by) % devices) for i in range(devices)])  7.3 us
    unnamed x16, local copies, waits for them, and re-layouts  5.38 us
    pallas_call x1, Pallas kernels, pack(): pl.pallas_call(pack_kernel, grid_spec=pltpu.PrefetchScalarGridSpec(num_sc...  3.54 us
  transfers between devices with their start and end apart: 5, of which 1 were waited for; matrix products, arithmetic and copies ran while one was open for 2% of the time, Pallas kernels for 6%

profile of v2, /device:TPU:1, one launch (start us, length us, event | category | flops | bytes accessed | tf_op | source)
XLA Modules:
  0.0 90.1 jit_solution(15510579435712841330)
XLA Ops:
  0.6 0.8 fusion.17
  1.4 1.6 %copy-done.3 = bf16[64,2,64,128]{3,2,1,0:T(8,128)(2,1)S(1)} copy-done((bf16[64,2,64,128]{3,2,1,0:T(8,128)(2,1)S(1)}, bf16[64,2,64,128]{3,2,1,0:T(8,128)(2,1)}, u32[]{:S(2)}) %copy-start.3) | copy-done | bytes 2097176
  3.0 3.5 %pack_pages.1 = bf16[64,2,64,128]{3,2,1,0:T(8,128)(2,1)S(1)} custom-call(s32[64]{0:T(128)S(1)} %get-tuple-element.19.slots_ref, bf16[64,2,64,128]{3,2,1,0:T(8,128)(2,1)S(1)} %copy-done.3), custom_call_target="tpu_custom_call" | custom-call | bytes 4194304 | tf_op jit(solution)/shard_map/pack_pages/pallas_call | solution.py:50
  6.5 0.0 copy-start
  6.5 1.3 %copy-done = bf16[64,2,64,128]{3,2,1,0:T(8,128)(2,1)} copy-done((bf16[64,2,64,128]{3,2,1,0:T(8,128)(2,1)}, bf16[64,2,64,128]{3,2,1,0:T(8,128)(2,1)S(1)}, u32[]{:S(2)}) %copy-start) | copy-done | bytes 2097176
  7.9 15.0 %all-to-all-start = ((bf16[64,2,64,128]{3,2,1,0:T(8,128)(2,1)}), bf16[64,2,64,128]{3,2,1,0:T(8,128)(2,1)S(1)}, u32[]{:S(2)}, u32[]{:S(2)}) async-start(bf16[64,2,64,128]{3,2,1,0:T(8,128)(2,1)} %copy-done), calls=%async_computation | async-start | bytes 4194304 | tf_op jit(solution)/shard_map/all_to_all | solution.py:284
  22.9 2.4 %collective-permute-start.1 = (bf16[2,2,64,128]{3,2,0,1:T(8,128)(2,1)S(1)}, bf16[2,2,64,128]{3,2,0,1:T(8,128)(2,1)S(1)}, u32[]{:S(2)}, u32[]{:S(2)}) collective-permute-start(bf16[2,2,64,128]{3,2,0,1:T(8,128)(2,1)S(1)} %copy.19), channel_id=1, source_target_pairs={{0,1},{1,0},{2,3},{3,2},{4,5},{5,4},{6,7},{7,6},{8,9},{9,8},{10,11... | collective-permute-start | bytes 196616 | tf_op jit(solution)/shard_map/ppermute | solution.py:24
  25.3 2.0 %collective-permute-start = (bf16[128,512]{1,0:T(8,128)(2,1)S(1)}, bf16[128,512]{1,0:T(8,128)(2,1)S(1)}, u32[]{:S(2)}, u32[]{:S(2)}) collective-permute-start(bf16[128,512]{1,0:T(8,128)(2,1)S(1)} %get-tuple-element.15), channel_id=1, source_target_pairs={{0,1},{1,0},{2,3},{3,2},{4,5},{5,4},{6,7},{7,6},{8,9},{9,8},{10,11... | collective-permute-start | bytes 393224 | tf_op jit(solution)/shard_map/ppermute | solution.py:24
  27.3 0.2 dynamic-slice_reduce_fusion
  27.5 0.1 fusion.19
  27.6 0.1 dynamic-slice_multiply_fusion
  27.7 0.1 add_convert_fusion
  27.8 0.1 broadcast_multiply_fusion
  27.9 0.2 cosine_bitcast_fusion
  28.1 0.2 fusion.21
  28.4 0.1 pad_maximum_fusion.1
  28.5 0.0 collective-permute-done.1
  28.5 0.3 bitcast_select_fusion
  28.9 7.3 %collective-permute-start.2 = (bf16[2,2,64,128]{3,2,1,0:T(8,128)(2,1)S(1)}, bf16[2,2,64,128]{3,2,1,0:T(8,128)(2,1)S(1)}, u32[]{:S(2)}, u32[]{:S(2)}) collective-permute-start(bf16[2,2,64,128]{3,2,1,0:T(8,128)(2,1)S(1)} %pad_maximum_fusion.3), channel_id=1, source_target_pairs={{0,256},{16,272},{32,288},{48,304},{64,320},{80,336},{96,352},{112... | collective-permute-start | bytes 196616 | tf_op jit(solution)/shard_map/ppermute | solution.py:29
  36.2 0.3 fusion.13
  36.6 0.0 collective-permute-done
  36.6 1.0 %prepare_queries.1 = (bf16[2,512,256]{2,1,0:T(8,128)(2,1)S(1)}, f32[2,512,256]{2,1,0:T(8,128)S(1)}) custom-call(bf16[2,128,512]{2,1,0:T(8,128)(2,1)S(1)} %pad_maximum_fusion.q_ref, f32[128,128]{1,0:T(8,128)S(1)} %get-tuple-element.21.cos_ref, f32[128,128]{1,0:T(8,128)S(1)} %get-tuple-element.22.sin_ref, bf16[128,128]{1,0:T(8,128)(2,1)S(1)} %fusion.15.keys_ref, ...), custom_call_target="tpu_custom_call" | custom-call | flops 67108864 | bytes 1572864 | tf_op jit(solution)/shard_map/prepare_queries/pallas_call | solution.py:108
  37.6 0.8 copy-done.1
  38.4 36.2 %collective-permute-done.2 = bf16[2,2,64,128]{3,2,1,0:T(8,128)(2,1)S(1)} collective-permute-done((bf16[2,2,64,128]{3,2,1,0:T(8,128)(2,1)S(1)}, bf16[2,2,64,128]{3,2,1,0:T(8,128)(2,1)S(1)}, u32[]{:S(2)}, u32[]{:S(2)}) %collective-permute-start.2) | collective-permute-done | bytes 65568 | tf_op jit(solution)/shard_map/ppermute | solution.py:29
  74.6 0.0 all-to-all-done
  74.6 1.0 %copy-done.2 = bf16[2,512,256]{2,1,0:T(8,128)(2,1)S(1)} copy-done((bf16[2,512,256]{2,1,0:T(8,128)(2,1)S(1)}, bf16[2,512,256]{2,1,0:T(8,128)(2,1)}, u32[]{:S(2)}) %copy-start.2) | copy-done | bytes 524312
  75.7 4.1 %attend_pages.3 = bf16[128,512]{1,0:T(8,128)(2,1)S(1)} custom-call(s32[32]{0:T(128)S(1)} %convert_element_type.40.live_ref, bf16[2,512,256]{2,1,0:T(8,128)(2,1)S(1)} %copy-done.2, f32[2,512,256]{2,1,0:T(8,128)S(1)} %get-tuple-element.7.state_ref, bf16[32,2,2,64,128]{4,3,2,1,0:T(8,128)(2,1)S(1)} %bitcast.65, bf16[128,128]{1,0:T(8,128)(2,1)S(1)} %fusion.15.keys_ref, ...), custom_call_target="tpu_custom_call" | custom-call | flops 1073741824 | bytes 2097152 | tf_op jit(solution)/shard_map/attend_pages/pallas_call | solution.py:241
  79.8 4.8 %collective-permute-start.3 = (bf16[128,512]{1,0:T(8,128)(2,1)S(1)}, bf16[128,512]{1,0:T(8,128)(2,1)S(1)}, u32[]{:S(2)}, u32[]{:S(2)}) collective-permute-start(bf16[128,512]{1,0:T(8,128)(2,1)S(1)} %attend_pages.3), channel_id=1, source_target_pairs={{0,1},{1,0},{2,3},{3,2},{4,5},{5,4},{6,7},{7,6},{8,9},{9,8},{10,11... | collective-permute-start | bytes 393224 | tf_op jit(solution)/shard_map/ppermute | solution.py:24
  84.6 4.1 %attend_pages.2 = bf16[128,512]{1,0:T(8,128)(2,1)S(1)} custom-call(s32[32]{0:T(128)S(1)} %convert_element_type.40.live_ref, bf16[2,512,256]{2,1,0:T(8,128)(2,1)S(1)} %copy-done.2, f32[2,512,256]{2,1,0:T(8,128)S(1)} %get-tuple-element.7.state_ref, bf16[32,2,2,64,128]{4,3,2,1,0:T(8,128)(2,1)S(1)} %bitcast.67, bf16[128,128]{1,0:T(8,128)(2,1)S(1)} %fusion.15.keys_ref, ...), custom_call_target="tpu_custom_call" | custom-call | flops 1073741824 | bytes 2097152 | tf_op jit(solution)/shard_map/attend_pages/pallas_call | solution.py:241
  88.7 0.0 collective-permute-done.3
  88.7 0.7 maximum_select_fusion
  89.4 0.6 copy.28
  (21 shorter events, 0.1 us)
Async XLA Ops:
  1.4 1.6 %copy-start.3 = (bf16[64,2,64,128]{3,2,1,0:T(8,128)(2,1)S(1)}, bf16[64,2,64,128]{3,2,1,0:T(8,128)(2,1)}, u32[]{:S(2)}) copy-start(bf16[64,2,64,128]{3,2,1,0:T(8,128)(2,1)} %pool_ref.1) | copy-start | bytes 6291460
  6.5 1.3 %copy-start = (bf16[64,2,64,128]{3,2,1,0:T(8,128)(2,1)}, bf16[64,2,64,128]{3,2,1,0:T(8,128)(2,1)S(1)}, u32[]{:S(2)}) copy-start(bf16[64,2,64,128]{3,2,1,0:T(8,128)(2,1)S(1)} %pack_pages.1) | copy-start | bytes 6291460
  7.9 15.0 %copy-start.5 = (bf16[2,2,64,128]{3,2,1,0:T(8,128)(2,1)S(1)}, bf16[2,2,64,128]{3,2,1,0:T(8,128)(2,1)}, u32[]{:S(2)}) copy-start(bf16[2,2,64,128]{3,2,1,0:T(8,128)(2,1)} %param.7) | copy-start | bytes 196612
  7.9 17.4 %copy-start.4 = (bf16[2,128,512]{2,1,0:T(8,128)(2,1)S(1)}, bf16[2,128,512]{2,1,0:T(8,128)(2,1)}, u32[]{:S(2)}) copy-start(bf16[2,128,512]{2,1,0:T(8,128)(2,1)} %param.6) | copy-start | bytes 786436
  7.9 19.7 %copy-start.6 = (s32[64]{0:T(128)S(1)}, s32[64]{0:T(128)}, u32[]{:S(2)}) copy-start(s32[64]{0:T(128)} %param.9) | copy-start | bytes 772
  7.9 66.7 %all-to-all-start = ((bf16[64,2,64,128]{3,2,1,0:T(8,128)(2,1)}), bf16[64,2,64,128]{3,2,1,0:T(8,128)(2,1)S(1)}, u32[]{:S(2)}, u32[]{:S(2)}) async-start(bf16[64,2,64,128]{3,2,1,0:T(8,128)(2,1)} %copy-done), calls=%async_computation | async-start | bytes 4194304 | tf_op jit(solution)/shard_map/all_to_all | solution.py:284
  22.9 5.6 %collective-permute-start.1 = (bf16[2,2,64,128]{3,2,0,1:T(8,128)(2,1)S(1)}, bf16[2,2,64,128]{3,2,0,1:T(8,128)(2,1)S(1)}, u32[]{:S(2)}, u32[]{:S(2)}) collective-permute-start(bf16[2,2,64,128]{3,2,0,1:T(8,128)(2,1)S(1)} %copy.19), channel_id=1, source_target_pairs={{0,1},{1,0},{2,3},{3,2},{4,5},{5,4},{6,7},{7,6},{8,9},{9,8},{10,11... | collective-permute-start | bytes 196616 | tf_op jit(solution)/shard_map/ppermute | solution.py:24
  25.3 11.3 %collective-permute-start = (bf16[128,512]{1,0:T(8,128)(2,1)S(1)}, bf16[128,512]{1,0:T(8,128)(2,1)S(1)}, u32[]{:S(2)}, u32[]{:S(2)}) collective-permute-start(bf16[128,512]{1,0:T(8,128)(2,1)S(1)} %get-tuple-element.15), channel_id=1, source_target_pairs={{0,1},{1,0},{2,3},{3,2},{4,5},{5,4},{6,7},{7,6},{8,9},{9,8},{10,11... | collective-permute-start | bytes 393224 | tf_op jit(solution)/shard_map/ppermute | solution.py:24
  28.9 45.8 %collective-permute-start.2 = (bf16[2,2,64,128]{3,2,1,0:T(8,128)(2,1)S(1)}, bf16[2,2,64,128]{3,2,1,0:T(8,128)(2,1)S(1)}, u32[]{:S(2)}, u32[]{:S(2)}) collective-permute-start(bf16[2,2,64,128]{3,2,1,0:T(8,128)(2,1)S(1)} %pad_maximum_fusion.3), channel_id=1, source_target_pairs={{0,256},{16,272},{32,288},{48,304},{64,320},{80,336},{96,352},{112... | collective-permute-start | bytes 196616 | tf_op jit(solution)/shard_map/ppermute | solution.py:29
  37.6 0.8 copy-start.1
  74.6 1.0 %copy-start.2 = (bf16[2,512,256]{2,1,0:T(8,128)(2,1)S(1)}, bf16[2,512,256]{2,1,0:T(8,128)(2,1)}, u32[]{:S(2)}) copy-start(bf16[2,512,256]{2,1,0:T(8,128)(2,1)} %copy-done.1) | copy-start | bytes 1572868
  79.8 8.9 %collective-permute-start.3 = (bf16[128,512]{1,0:T(8,128)(2,1)S(1)}, bf16[128,512]{1,0:T(8,128)(2,1)S(1)}, u32[]{:S(2)}, u32[]{:S(2)}) collective-permute-start(bf16[128,512]{1,0:T(8,128)(2,1)S(1)} %attend_pages.3), channel_id=1, source_target_pairs={{0,1},{1,0},{2,3},{3,2},{4,5},{5,4},{6,7},{7,6},{8,9},{9,8},{10,11... | collective-permute-start | bytes 393224 | tf_op jit(solution)/shard_map/ppermute | solution.py:24

commit v3 on v2

--- a/solution.py
+++ b/solution.py
@@ -12,8 +12,8 @@
 MIB = 1024 * 1024
 GROUP = ("pool", "core")
 CONTRACT_LAST = (((1,), (1,)), ((), ()))
-GROUPED = 4
-STEPS = 4
+GROUPED = 8
+UNROLL = 4
 
 
 def factor_of(width):
@@ -35,34 +35,47 @@
     return positions.astype(jnp.float32)[:, None] * inverse[None, :]
 
 
-def pack_kernel(slots_ref, pool_ref, out_ref, sem):
+def pack_kernel(table_ref, pool_ref, out_ref, slots_ref, scalars_ref, sem):
     count = out_ref.shape[0]
+    slot_count = pool_ref.shape[0]
+    slot = table_ref[...] - lax.axis_index("pool") * slot_count
+    mine = jnp.logical_and(slot >= 0, slot < slot_count)
+    slots_ref[...] = jnp.sum(jnp.where(mine, slot, 0), axis=0, keepdims=True)
+    copy = pltpu.make_async_copy(slots_ref, scalars_ref, sem.at[0])
+    copy.start()
+    copy.wait()
 
     @pl.loop(0, count, unroll=8)
     def _(r):
-        pltpu.make_async_copy(pool_ref.at[slots_ref[r]], out_ref.at[r], sem).start()
-
-    pltpu.make_async_copy(out_ref, out_ref, sem).wait()
-
-
-def pack(slots, pool_kv):
-    shape = (slots.shape[0],) + pool_kv.shape[1:]
+        pltpu.make_async_copy(
+            pool_ref.at[scalars_ref[0, r]], out_ref.at[r], sem.at[1]
+        ).start()
+
+    pltpu.make_async_copy(out_ref, out_ref, sem.at[1]).wait()
+
+
+def pack(page_table, pool_kv):
+    requests, most = page_table.shape
+    shape = (requests,) + pool_kv.shape[1:]
     return pl.pallas_call(
         pack_kernel,
-        grid_spec=pltpu.PrefetchScalarGridSpec(
-            num_scalar_prefetch=1,
-            grid=(1,),
-            in_specs=[pl.BlockSpec(memory_space=pl.ANY)],
-            out_specs=pl.BlockSpec(memory_space=pl.ANY),
-            scratch_shapes=[pltpu.SemaphoreType.DMA],
-        ),
+        in_specs=[
+            pl.BlockSpec(memory_space=pltpu.VMEM),
+            pl.BlockSpec(memory_space=pltpu.HBM),
+        ],
+        out_specs=pl.BlockSpec(memory_space=pltpu.HBM),
+        scratch_shapes=[
+            pltpu.VMEM((1, requests), jnp.int32),
+            pltpu.SMEM((1, requests), jnp.int32),
+            pltpu.SemaphoreType.DMA((2,)),
+        ],
         out_shape=jax.ShapeDtypeStruct(shape, pool_kv.dtype),
         compiler_params=pltpu.CompilerParams(vmem_limit_bytes=2 * MIB),
         cost_estimate=pl.CostEstimate(
             flops=0, bytes_accessed=4 * math.prod(shape), transcendentals=0
         ),
         name="pack_pages",
-    )(slots, pool_kv)
+    )(page_table.T, pool_kv)
 
 
 def own_scores(rq, fresh_keys, tokens):
@@ -130,80 +143,79 @@
     )(q, cosine, sine, fresh_keys, fresh_values)
 
 
-def attend_kernel(heads, factor, live_ref, rq_ref, state_ref, kv_ref, keys_ref, values_ref,
-                  all_ref, out_ref, acc_ref, page_ref, top_ref, sem):
-    step = pl.program_id(0)
+def attend_kernel(heads, factor, landing, live_ref, rq_ref, state_ref, all_ref, keys_ref,
+                  values_ref, *refs):
+    if landing:
+        landed_ref, whole_ref, placed_ref, acc_ref, top_ref, out_ref, sem = refs
+        place = pltpu.make_async_copy(landed_ref, placed_ref, sem.at[0])
+        place.start()
+    else:
+        out_ref, acc_ref, top_ref = refs
     tokens, wide = out_ref.shape
     width = wide // heads
-    rows = heads * tokens
-    page = kv_ref.shape[4]
-    count = kv_ref.shape[0]
-    first = step * count
-
-    @pl.when(step == 0)
-    def _():
-        acc_ref[...] = state_ref[0]
-
+    page = all_ref.shape[4]
+    pages = all_ref.shape[0]
     row = lax.broadcasted_iota(jnp.int32, (width, page), 0)
 
     def flags(p):
         hidden = jnp.where(live_ref[p] > 0, 0.0, -1e30)
         return jnp.where(row == 0, 1.0, jnp.where(row == 1, hidden, 0.0)).astype(jnp.bfloat16)
 
+    def part_of(p, which):
+        return jnp.concatenate([all_ref[p, 0, which], all_ref[p, 1, which]], axis=0)
+
     ones = jnp.ones((width, GROUPED * page), jnp.bfloat16)
-    rq = rq_ref[0]
-    for at in range(0, count, GROUPED):
-        weights, values = [], []
-        for p in range(at, at + GROUPED, 2):
+    acc_ref[...] = state_ref[int(landing)]
+    rq = rq_ref[int(landing)]
+
+    @pl.loop(0, pages // GROUPED, unroll=UNROLL)
+    def _(g):
+        at = g * GROUPED
+        weights = []
+        for i in range(0, GROUPED, 2):
             keys = jnp.concatenate(
                 [
-                    jnp.concatenate(
-                        [kv_ref[p + i, 0, 0], kv_ref[p + i, 1, 0], flags(first + p + i)], axis=0
-                    )
-                    for i in range(2)
+                    jnp.concatenate([part_of(at + i + j, 0), flags(at + i + j)], axis=0)
+                    for j in range(2)
                 ],
                 axis=1,
             )
             s = jnp.dot(rq, keys, preferred_element_type=jnp.float32)
             weights.append(jnp.exp2(s * factor).astype(jnp.bfloat16))
-        for p in range(at, at + GROUPED):
-            values.append(jnp.concatenate([kv_ref[p, 0, 1], kv_ref[p, 1, 1]], axis=0))
-        block = jnp.concatenate([jnp.concatenate(values, axis=1), ones], axis=0)
+        values = jnp.concatenate([part_of(at + i, 1) for i in range(GROUPED)], axis=1)
         acc_ref[...] += lax.dot_general(
-            jnp.concatenate(weights, axis=1), block, CONTRACT_LAST,
-            preferred_element_type=jnp.float32,
+            jnp.concatenate(weights, axis=1), jnp.concatenate([values, ones], axis=0),
+            CONTRACT_LAST, preferred_element_type=jnp.float32,
         )
 
-    @pl.when(step == pl.num_programs(0) - 1)
+    @pl.when(jnp.logical_not(jnp.max(acc_ref[:, width:]) <= 1e30))
     def _():
-        largest_total = jnp.max(acc_ref[:, width:])
-
-        @pl.when(jnp.logical_not(largest_total <= 1e30))
-        def _():
-            exact(factor, tokens, width, live_ref, rq_ref, keys_ref, values_ref, all_ref,
-                  acc_ref, page_ref, top_ref, sem)
-
-        done = (acc_ref[:, :width] / acc_ref[:, width:]).astype(jnp.bfloat16)
-        for h in range(heads):
-            out_ref[:, h * width:(h + 1) * width] = done[h * tokens:(h + 1) * tokens, :]
-
-
-def exact(factor, tokens, width, live_ref, rq_ref, keys_ref, values_ref, all_ref,
-          acc_ref, page_ref, top_ref, sem):
-    rows = rq_ref.shape[1]
+        exact(factor, tokens, width, live_ref, rq_ref.at[int(landing)], keys_ref, values_ref,
+              all_ref, acc_ref, top_ref)
+
+    done = (acc_ref[:, :width] / acc_ref[:, width:]).astype(jnp.bfloat16)
+    for h in range(heads):
+        out_ref[:, h * width:(h + 1) * width] = done[h * tokens:(h + 1) * tokens, :]
+    if landing:
+        keep = pltpu.make_async_copy(out_ref, whole_ref.at[lax.axis_index("core")], sem.at[1])
+        keep.start()
+        keep.wait()
+        place.wait()
+
+
+def exact(factor, tokens, width, live_ref, rq_ref, keys_ref, values_ref, all_ref, acc_ref, top_ref):
+    rows = rq_ref.shape[0]
     pages = all_ref.shape[0]
-    half = width // 2
-    rq = rq_ref[0, :, :width]
+    rq = rq_ref[:, :width]
     own = own_scores(rq, keys_ref[...], tokens)
     top_ref[...] = own
 
+    def part_of(p, which):
+        return jnp.concatenate([all_ref[p, 0, which], all_ref[p, 1, which]], axis=0)
+
     def scores_of(p):
-        copy = pltpu.make_async_copy(all_ref.at[p], page_ref, sem)
-        copy.start()
-        copy.wait()
-        keys = jnp.concatenate([page_ref[0, 0], page_ref[1, 0]], axis=0)
         hidden = jnp.where(live_ref[p] > 0, 0.0, -1e30)
-        return jnp.dot(rq, keys, preferred_element_type=jnp.float32) + hidden
+        return jnp.dot(rq, part_of(p, 0), preferred_element_type=jnp.float32) + hidden
 
     @pl.loop(0, pages)
     def _(p):
@@ -222,52 +234,49 @@
     @pl.loop(0, pages)
     def _(p):
         w = jnp.exp2((scores_of(p) - top_ref[...]) * factor)
-        values = jnp.concatenate([page_ref[0, 1], page_ref[1, 1]], axis=0)
         acc_ref[:, :width] += lax.dot_general(
-            w.astype(jnp.bfloat16), values, CONTRACT_LAST, preferred_element_type=jnp.float32
+            w.astype(jnp.bfloat16), part_of(p, 1), CONTRACT_LAST, preferred_element_type=jnp.float32
         )
         acc_ref[:, width:] += jnp.broadcast_to(
             jnp.sum(w, axis=1, keepdims=True), (rows, width)
         )
 
 
-def attend(which, tokens, live, rq, state, arrived, fresh_keys, fresh_values):
+def attend(tokens, live, rq, state, arrived, fresh_keys, fresh_values, landed=None):
     _, rows, double = rq.shape
     pages, _, _, half, page = arrived.shape
     width = double // 2
     heads = rows // tokens
-    steps = STEPS
-    per = pages // steps
+    shape = (tokens, heads * width)
+    landing = landed is not None
+    vmem = pl.BlockSpec(memory_space=pltpu.VMEM)
+    hbm = pl.BlockSpec(memory_space=pltpu.HBM)
+    scratch = [pltpu.VMEM((rows, double), jnp.float32), pltpu.VMEM((rows, page), jnp.float32)]
+    if landing:
+        more, more_specs = [landed], [vmem]
+        out_shape = [
+            jax.ShapeDtypeStruct((2,) + shape, jnp.bfloat16),
+            jax.ShapeDtypeStruct(landed.shape, landed.dtype),
+        ]
+        out_specs = [hbm, hbm]
+        scratch += [pltpu.VMEM(shape, jnp.bfloat16), pltpu.SemaphoreType.DMA((2,))]
+    else:
+        more, more_specs = [], []
+        out_shape, out_specs = jax.ShapeDtypeStruct(shape, jnp.bfloat16), vmem
     return pl.pallas_call(
-        functools.partial(attend_kernel, heads, factor_of(width)),
-        grid_spec=pltpu.PrefetchScalarGridSpec(
-            num_scalar_prefetch=1,
-            grid=(steps,),
-            in_specs=[
-                pl.BlockSpec((1, rows, double), lambda s, *_: (which, 0, 0)),
-                pl.BlockSpec((1, rows, double), lambda s, *_: (which, 0, 0)),
-                pl.BlockSpec((per, 2, 2, half, page), lambda s, *_: (s, 0, 0, 0, 0)),
-                pl.BlockSpec((width, page), lambda s, *_: (0, 0)),
-                pl.BlockSpec((width, page), lambda s, *_: (0, 0)),
-                pl.BlockSpec(memory_space=pl.ANY),
-            ],
-            out_specs=pl.BlockSpec((tokens, heads * width), lambda s, *_: (0, 0)),
-            scratch_shapes=[
-                pltpu.VMEM((rows, double), jnp.float32),
-                pltpu.VMEM((2, 2, half, page), jnp.bfloat16),
-                pltpu.VMEM((rows, page), jnp.float32),
-                pltpu.SemaphoreType.DMA,
-            ],
-        ),
-        out_shape=jax.ShapeDtypeStruct((tokens, heads * width), jnp.bfloat16),
-        compiler_params=pltpu.CompilerParams(vmem_limit_bytes=40 * MIB),
+        functools.partial(attend_kernel, heads, factor_of(width), landing),
+        in_specs=[pl.BlockSpec(memory_space=pltpu.SMEM)] + [vmem] * 5 + more_specs,
+        out_specs=out_specs,
+        scratch_shapes=scratch,
+        out_shape=out_shape,
+        compiler_params=pltpu.CompilerParams(vmem_limit_bytes=24 * MIB),
         cost_estimate=pl.CostEstimate(
             flops=4 * rows * pages * page * width,
             bytes_accessed=pages * width * page * 4,
             transcendentals=rows * pages * page,
         ),
-        name="attend_pages",
-    )(live, rq, state, arrived, fresh_keys, fresh_values, arrived)
+        name="attend_kept" if landing else "attend_sent",
+    )(live, rq, state, arrived, fresh_keys, fresh_values, *more)
 
 
 def on_device(pool_kv, queries, new_kv, page_table, prefix_pages):
@@ -279,10 +288,8 @@
     head_width = 2 * half_width
     local_requests, suffix_len, _ = queries.shape
     owner_of = page_table // slot_count
-    slot_of = jnp.sum(jnp.where(owner_of == pool_rank, page_table % slot_count, 0), axis=1)
-
     arrived = lax.all_to_all(
-        pack(slot_of, pool_kv), GROUP, split_axis=0, concat_axis=0, tiled=True
+        pack(page_table, pool_kv), GROUP, split_axis=0, concat_axis=0, tiled=True
     ).reshape(pool_count, 2, 2, half_width, page_len)
 
     first_row = pool_rank * local_requests
@@ -330,16 +337,11 @@
     rq, state = prepare(
         jnp.stack([taken, kept], axis=0), q_cosine, q_sine, fresh_keys, fresh_values
     )
-    arrived, landed = lax.optimization_barrier((arrived, landed))
     inputs = (live, rq, state, arrived, fresh_keys, fresh_values)
-    for_partner = attend(0, suffix_len, *inputs)
+    for_partner = attend(suffix_len, *inputs)
     from_partner = swap_cores(for_partner)
-    stays = attend(1, suffix_len, *inputs)
-    attended = jnp.where(
-        lower_half,
-        jnp.stack([stays, from_partner], axis=0),
-        jnp.stack([from_partner, stays], axis=0),
-    )
+    attended, landed = attend(suffix_len, *inputs, landed)
+    attended = lax.dynamic_update_index_in_dim(attended, from_partner, 1 - core, 0)
     return (attended, landed)
 
 

time: 90.5 us -> 82.3 us (0.909)
  Pallas kernels: 12.8 us -> 9.91 us
  waiting for transfers between devices: 36.2 us -> 33.9 us
  other arithmetic: 2.93 us -> 1.65 us
  starting transfers between devices: 31.4 us -> 30.2 us
    ppermute x1, waiting for transfers between devices: 36.2 us -> 0.01 us  [from_behind(): lax.ppermute(array, axis, [(i, (i + by) % devices) for i in range(devices)])]
    all_to_all x1, waiting for transfers between devices: 0.01 us -> 33.9 us  [on_device(): lax.all_to_all(pack(page_table, pool_kv), GROUP, split_axis=0, concat_axi...]
    pallas_call x3, Pallas kernels: 11.8 us -> 8.9 us  [the longest x2 6.99 us: attend(): pl.pallas_call(functools.partial(attend_kernel, heads, factor_of(width),...]
    unnamed x16 -> x17, local copies, waits for them, and re-layouts: 5.38 us -> 4.17 us
    ppermute x3, starting transfers between devices: 9.1 us -> 7.95 us  [swap_cores(): return lax.ppermute(array, 'core', [(0, 1), (1, 0)])]
  transfers between devices with their start and end apart: 5 -> 5, of which waited for: 1 -> 1; matrix products, arithmetic and copies ran while one was open for 2% -> 2% of each run, Pallas kernels for 6% -> 10%
where the time goes in v3:
time: 82.3 us; the launch traced here: 81.8 us
  waiting for transfers between devices  33.9 us (41%)
  starting transfers between devices  30.2 us (37%)
  Pallas kernels  9.91 us (12%)
  local copies, waits for them, and re-layouts  5.13 us (6%)
  other arithmetic  1.65 us (2%)
  between operations  0.98 us (1%)
    all_to_all x1, waiting for transfers between devices, on_device(): lax.all_to_all(pack(page_table, pool_kv), GROUP, split_axis=0, concat_axi...  33.9 us
    all_to_all x1, starting transfers between devices, on_device(): lax.all_to_all(pack(page_table, pool_kv), GROUP, split_axis=0, concat_axi...  15 us
    ppermute x3, starting transfers between devices, swap_cores(): return lax.ppermute(array, 'core', [(0, 1), (1, 0)])  7.95 us
    ppermute x1, starting transfers between devices, from_behind(): lax.ppermute(array, axis, [(i, (i + by) % devices) for i in range(devices)])  7.3 us
    pallas_call x2, Pallas kernels, attend(): pl.pallas_call(functools.partial(attend_kernel, heads, factor_of(width),...  6.99 us
    unnamed x17, local copies, waits for them, and re-layouts  4.17 us
    pallas_call x1, Pallas kernels, pack(): pl.pallas_call(pack_kernel, in_specs=[pl.BlockSpec(memory_space=pltpu.VME...  1.91 us
  transfers between devices with their start and end apart: 5, of which 1 were waited for; matrix products, arithmetic and copies ran while one was open for 2% of the time, Pallas kernels for 10%

profile of v3, /device:TPU:1, one launch (start us, length us, event | category | flops | bytes accessed | tf_op | source)
XLA Modules:
  0.0 81.8 jit_solution(10548817805085827900)
XLA Ops:
  0.6 1.6 %copy-done = bf16[64,2,64,128]{3,2,1,0:T(8,128)(2,1)S(1)} copy-done((bf16[64,2,64,128]{3,2,1,0:T(8,128)(2,1)S(1)}, bf16[64,2,64,128]{3,2,1,0:T(8,128)(2,1)}, u32[]{:S(2)}) %copy-start) | copy-done | bytes 2097176
  2.2 0.7 copy-done.1
  2.9 1.9 %pack_pages.1 = bf16[64,2,64,128]{3,2,1,0:T(8,128)(2,1)} custom-call(s32[32,64]{1,0:T(8,128)S(1)} %bitcast.68, bf16[64,2,64,128]{3,2,1,0:T(8,128)(2,1)S(1)} %copy-done), custom_call_target="tpu_custom_call" | custom-call | bytes 4194304 | tf_op jit(solution)/shard_map/pack_pages/pallas_call | solution.py:60
  4.9 0.0 copy-start.6
  4.9 0.0 copy-start.5
  4.9 0.0 copy-start.2
  4.9 0.0 copy-start.7
  4.9 15.0 %all-to-all-start = ((bf16[64,2,64,128]{3,2,1,0:T(8,128)(2,1)}), bf16[64,2,64,128]{3,2,1,0:T(8,128)(2,1)S(1)}, u32[]{:S(2)}, u32[]{:S(2)}) async-start(bf16[64,2,64,128]{3,2,1,0:T(8,128)(2,1)} %pack_pages.1), calls=%async_computation | async-start | bytes 4194304 | tf_op jit(solution)/shard_map/all_to_all | solution.py:291
  19.9 2.4 %collective-permute-start.1 = (bf16[2,2,64,128]{3,2,0,1:T(8,128)(2,1)S(1)}, bf16[2,2,64,128]{3,2,0,1:T(8,128)(2,1)S(1)}, u32[]{:S(2)}, u32[]{:S(2)}) collective-permute-start(bf16[2,2,64,128]{3,2,0,1:T(8,128)(2,1)S(1)} %copy.19), channel_id=1, source_target_pairs={{0,1},{1,0},{2,3},{3,2},{4,5},{5,4},{6,7},{7,6},{8,9},{9,8},{10,11... | collective-permute-start | bytes 196616 | tf_op jit(solution)/shard_map/ppermute | solution.py:24
  22.3 2.0 %collective-permute-start = (bf16[128,512]{1,0:T(8,128)(2,1)S(1)}, bf16[128,512]{1,0:T(8,128)(2,1)S(1)}, u32[]{:S(2)}, u32[]{:S(2)}) collective-permute-start(bf16[128,512]{1,0:T(8,128)(2,1)S(1)} %get-tuple-element.15), channel_id=1, source_target_pairs={{0,1},{1,0},{2,3},{3,2},{4,5},{5,4},{6,7},{7,6},{8,9},{9,8},{10,11... | collective-permute-start | bytes 393224 | tf_op jit(solution)/shard_map/ppermute | solution.py:24
  24.4 0.2 fusion.17
  24.6 0.1 fusion.19
  24.7 0.1 dynamic-slice_multiply_fusion
  24.8 0.1 add_convert_fusion
  24.9 0.1 broadcast_multiply_fusion
  25.0 0.2 cosine_bitcast_fusion
  25.2 0.2 fusion.21
  25.5 0.1 pad_maximum_fusion.1
  25.6 0.3 bitcast_select_fusion
  26.0 7.3 %collective-permute-start.2 = (bf16[2,2,64,128]{3,2,1,0:T(8,128)(2,1)S(1)}, bf16[2,2,64,128]{3,2,1,0:T(8,128)(2,1)S(1)}, u32[]{:S(2)}, u32[]{:S(2)}) collective-permute-start(bf16[2,2,64,128]{3,2,1,0:T(8,128)(2,1)S(1)} %pad_maximum_fusion.3), channel_id=1, source_target_pairs={{0,256},{16,272},{32,288},{48,304},{64,320},{80,336},{96,352},{112... | collective-permute-start | bytes 196616 | tf_op jit(solution)/shard_map/ppermute | solution.py:29
  33.3 0.3 fusion.13
  33.7 0.0 collective-permute-done
  33.7 1.0 %prepare_queries.1 = (bf16[2,512,256]{2,1,0:T(8,128)(2,1)S(1)}, f32[2,512,256]{2,1,0:T(8,128)S(1)}) custom-call(bf16[2,128,512]{2,1,0:T(8,128)(2,1)S(1)} %pad_maximum_fusion.q_ref, f32[128,128]{1,0:T(8,128)S(1)} %get-tuple-element.19.cos_ref, f32[128,128]{1,0:T(8,128)S(1)} %get-tuple-element.20.sin_ref, bf16[128,128]{1,0:T(8,128)(2,1)S(1)} %fusion.15.keys_ref, ...), custom_call_target="tpu_custom_call" | custom-call | flops 67108864 | bytes 1572864 | tf_op jit(solution)/shard_map/prepare_queries/pallas_call | solution.py:121
  34.7 0.8 copy-done.3
  35.5 33.9 %all-to-all-done = bf16[64,2,64,128]{3,2,1,0:T(8,128)(2,1)S(1)} async-done(((bf16[64,2,64,128]{3,2,1,0:T(8,128)(2,1)}), bf16[64,2,64,128]{3,2,1,0:T(8,128)(2,1)S(1)}, u32[]{:S(2)}, u32[]{:S(2)}) %all-to-all-start) | async-done | bytes 2097184 | tf_op jit(solution)/shard_map/all_to_all | solution.py:291
  69.5 1.0 %copy-done.4 = bf16[2,512,256]{2,1,0:T(8,128)(2,1)S(1)} copy-done((bf16[2,512,256]{2,1,0:T(8,128)(2,1)S(1)}, bf16[2,512,256]{2,1,0:T(8,128)(2,1)}, u32[]{:S(2)}) %copy-start.4) | copy-done | bytes 524312
  70.5 3.2 %attend_sent.1 = bf16[128,512]{1,0:T(8,128)(2,1)S(1)} custom-call(s32[32]{0:T(128)S(1)} %convert_element_type.40.live_ref, bf16[2,512,256]{2,1,0:T(8,128)(2,1)S(1)} %copy-done.4, f32[2,512,256]{2,1,0:T(8,128)S(1)} %get-tuple-element.7.state_ref, bf16[32,2,2,64,128]{4,3,2,1,0:T(8,128)(2,1)S(1)} %bitcast.66, bf16[128,128]{1,0:T(8,128)(2,1)S(1)} %fusion.15.keys_ref, ...), custom_call_target="tpu_custom_call" | custom-call | flops 1073741824 | bytes 2097152 | tf_op jit(solution)/shard_map/attend_sent/pallas_call | solution.py:266
  73.7 3.6 %collective-permute-start.3 = (bf16[128,512]{1,0:T(8,128)(2,1)S(1)}, bf16[128,512]{1,0:T(8,128)(2,1)S(1)}, u32[]{:S(2)}, u32[]{:S(2)}) collective-permute-start(bf16[128,512]{1,0:T(8,128)(2,1)S(1)} %attend_sent.1), channel_id=1, source_target_pairs={{0,1},{1,0},{2,3},{3,2},{4,5},{5,4},{6,7},{7,6},{8,9},{9,8},{10,11... | collective-permute-start | bytes 393224 | tf_op jit(solution)/shard_map/ppermute | solution.py:24
  77.3 0.0 collective-permute-done.2.refs_0_
  77.3 3.8 %attend_kept.1 = (bf16[2,128,512]{2,1,0:T(8,128)(2,1)}, bf16[2,2,64,128]{3,2,1,0:T(8,128)(2,1)}) custom-call(s32[32]{0:T(128)S(1)} %convert_element_type.40.live_ref, bf16[2,512,256]{2,1,0:T(8,128)(2,1)S(1)} %copy-done.4, f32[2,512,256]{2,1,0:T(8,128)S(1)} %get-tuple-element.7.state_ref, bf16[32,2,2,64,128]{4,3,2,1,0:T(8,128)(2,1)S(1)} %bitcast.67, ...), custom_call_target="tpu_custom_call" | custom-call | flops 1073741824 | bytes 2097152 | tf_op jit(solution)/shard_map/attend_kept/pallas_call | solution.py:266
  81.1 0.0 collective-permute-done.3
  81.2 0.7 bitcast_dynamic-update-slice_fusion
  (23 shorter events, 0.2 us)
Async XLA Ops:
  0.6 1.6 %copy-start = (bf16[64,2,64,128]{3,2,1,0:T(8,128)(2,1)S(1)}, bf16[64,2,64,128]{3,2,1,0:T(8,128)(2,1)}, u32[]{:S(2)}) copy-start(bf16[64,2,64,128]{3,2,1,0:T(8,128)(2,1)} %pool_ref.1) | copy-start | bytes 6291460
  2.2 0.7 copy-start.1
  4.9 15.0 %copy-start.6 = (bf16[2,2,64,128]{3,2,1,0:T(8,128)(2,1)S(1)}, bf16[2,2,64,128]{3,2,1,0:T(8,128)(2,1)}, u32[]{:S(2)}) copy-start(bf16[2,2,64,128]{3,2,1,0:T(8,128)(2,1)} %param.7) | copy-start | bytes 196612
  4.9 17.4 %copy-start.5 = (bf16[2,128,512]{2,1,0:T(8,128)(2,1)S(1)}, bf16[2,128,512]{2,1,0:T(8,128)(2,1)}, u32[]{:S(2)}) copy-start(bf16[2,128,512]{2,1,0:T(8,128)(2,1)} %param.6) | copy-start | bytes 786436
  4.9 19.5 %copy-start.2 = (s32[64,32]{0,1:T(8,128)S(1)}, s32[64,32]{0,1:T(8,128)}, u32[]{:S(2)}) copy-start(s32[64,32]{0,1:T(8,128)} %param.8) | copy-start | bytes 24580
  4.9 19.8 %copy-start.7 = (s32[64]{0:T(128)S(1)}, s32[64]{0:T(128)}, u32[]{:S(2)}) copy-start(s32[64]{0:T(128)} %param.9) | copy-start | bytes 772
  4.9 64.5 %all-to-all-start = ((bf16[64,2,64,128]{3,2,1,0:T(8,128)(2,1)}), bf16[64,2,64,128]{3,2,1,0:T(8,128)(2,1)S(1)}, u32[]{:S(2)}, u32[]{:S(2)}) async-start(bf16[64,2,64,128]{3,2,1,0:T(8,128)(2,1)} %pack_pages.1), calls=%async_computation | async-start | bytes 4194304 | tf_op jit(solution)/shard_map/all_to_all | solution.py:291
  19.9 5.7 %collective-permute-start.1 = (bf16[2,2,64,128]{3,2,0,1:T(8,128)(2,1)S(1)}, bf16[2,2,64,128]{3,2,0,1:T(8,128)(2,1)S(1)}, u32[]{:S(2)}, u32[]{:S(2)}) collective-permute-start(bf16[2,2,64,128]{3,2,0,1:T(8,128)(2,1)S(1)} %copy.19), channel_id=1, source_target_pairs={{0,1},{1,0},{2,3},{3,2},{4,5},{5,4},{6,7},{7,6},{8,9},{9,8},{10,11... | collective-permute-start | bytes 196616 | tf_op jit(solution)/shard_map/ppermute | solution.py:24
  22.3 11.3 %collective-permute-start = (bf16[128,512]{1,0:T(8,128)(2,1)S(1)}, bf16[128,512]{1,0:T(8,128)(2,1)S(1)}, u32[]{:S(2)}, u32[]{:S(2)}) collective-permute-start(bf16[128,512]{1,0:T(8,128)(2,1)S(1)} %get-tuple-element.15), channel_id=1, source_target_pairs={{0,1},{1,0},{2,3},{3,2},{4,5},{5,4},{6,7},{7,6},{8,9},{9,8},{10,11... | collective-permute-start | bytes 393224 | tf_op jit(solution)/shard_map/ppermute | solution.py:24
  26.0 51.3 %collective-permute-start.2 = (bf16[2,2,64,128]{3,2,1,0:T(8,128)(2,1)S(1)}, bf16[2,2,64,128]{3,2,1,0:T(8,128)(2,1)S(1)}, u32[]{:S(2)}, u32[]{:S(2)}) collective-permute-start(bf16[2,2,64,128]{3,2,1,0:T(8,128)(2,1)S(1)} %pad_maximum_fusion.3), channel_id=1, source_target_pairs={{0,256},{16,272},{32,288},{48,304},{64,320},{80,336},{96,352},{112... | collective-permute-start | bytes 196616 | tf_op jit(solution)/shard_map/ppermute | solution.py:29
  34.7 0.8 copy-start.3
  69.5 1.0 %copy-start.4 = (bf16[2,512,256]{2,1,0:T(8,128)(2,1)S(1)}, bf16[2,512,256]{2,1,0:T(8,128)(2,1)}, u32[]{:S(2)}) copy-start(bf16[2,512,256]{2,1,0:T(8,128)(2,1)} %copy-done.3) | copy-start | bytes 1572868
  73.7 7.5 %collective-permute-start.3 = (bf16[128,512]{1,0:T(8,128)(2,1)S(1)}, bf16[128,512]{1,0:T(8,128)(2,1)S(1)}, u32[]{:S(2)}, u32[]{:S(2)}) collective-permute-start(bf16[128,512]{1,0:T(8,128)(2,1)S(1)} %attend_sent.1), channel_id=1, source_target_pairs={{0,1},{1,0},{2,3},{3,2},{4,5},{5,4},{6,7},{7,6},{8,9},{9,8},{10,11... | collective-permute-start | bytes 393224 | tf_op jit(solution)/shard_map/ppermute | solution.py:24

commit v4 on v3

--- a/solution.py
+++ b/solution.py
@@ -13,11 +13,14 @@
 GROUP = ("pool", "core")
 CONTRACT_LAST = (((1,), (1,)), ((), ()))
 GROUPED = 8
-UNROLL = 4
 
 
 def factor_of(width):
     return math.log2(math.e) / math.sqrt(width)
+
+
+def in_hbm(array):
+    return pltpu.with_memory_space_constraint(array, pltpu.HBM)
 
 
 def swap_cores(array):
@@ -35,47 +38,55 @@
     return positions.astype(jnp.float32)[:, None] * inverse[None, :]
 
 
-def pack_kernel(table_ref, pool_ref, out_ref, slots_ref, scalars_ref, sem):
+def pack_kernel(table_ref, pool_ref, out_ref, held_ref, rows_ref, slots_ref, scalars_ref, sem):
     count = out_ref.shape[0]
     slot_count = pool_ref.shape[0]
-    slot = table_ref[...] - lax.axis_index("pool") * slot_count
+    table = pltpu.make_async_copy(table_ref, rows_ref, sem.at[0])
+    table.start()
+    part = slot_count // 8
+    for i in range(8):
+        span = pl.ds(i * part, part)
+        pltpu.make_async_copy(pool_ref.at[span], held_ref.at[span], sem.at[1]).start()
+    table.wait()
+    slot = rows_ref[...] - lax.axis_index("pool") * slot_count
     mine = jnp.logical_and(slot >= 0, slot < slot_count)
     slots_ref[...] = jnp.sum(jnp.where(mine, slot, 0), axis=0, keepdims=True)
-    copy = pltpu.make_async_copy(slots_ref, scalars_ref, sem.at[0])
+    copy = pltpu.make_async_copy(slots_ref, scalars_ref, sem.at[2])
     copy.start()
     copy.wait()
-
-    @pl.loop(0, count, unroll=8)
+    pltpu.make_async_copy(pool_ref, held_ref, sem.at[1]).wait()
+
+    @pl.loop(0, count, unroll=16)
     def _(r):
         pltpu.make_async_copy(
-            pool_ref.at[scalars_ref[0, r]], out_ref.at[r], sem.at[1]
+            held_ref.at[scalars_ref[0, r]], out_ref.at[r], sem.at[3]
         ).start()
 
-    pltpu.make_async_copy(out_ref, out_ref, sem.at[1]).wait()
+    pltpu.make_async_copy(out_ref, out_ref, sem.at[3]).wait()
 
 
 def pack(page_table, pool_kv):
     requests, most = page_table.shape
     shape = (requests,) + pool_kv.shape[1:]
+    hbm = pl.BlockSpec(memory_space=pltpu.HBM)
     return pl.pallas_call(
         pack_kernel,
-        in_specs=[
-            pl.BlockSpec(memory_space=pltpu.VMEM),
-            pl.BlockSpec(memory_space=pltpu.HBM),
-        ],
-        out_specs=pl.BlockSpec(memory_space=pltpu.HBM),
+        in_specs=[hbm, hbm],
+        out_specs=hbm,
         scratch_shapes=[
+            pltpu.VMEM(pool_kv.shape, pool_kv.dtype),
+            pltpu.VMEM((most, requests), jnp.int32),
             pltpu.VMEM((1, requests), jnp.int32),
             pltpu.SMEM((1, requests), jnp.int32),
-            pltpu.SemaphoreType.DMA((2,)),
+            pltpu.SemaphoreType.DMA((4,)),
         ],
         out_shape=jax.ShapeDtypeStruct(shape, pool_kv.dtype),
-        compiler_params=pltpu.CompilerParams(vmem_limit_bytes=2 * MIB),
+        compiler_params=pltpu.CompilerParams(vmem_limit_bytes=8 * MIB),
         cost_estimate=pl.CostEstimate(
             flops=0, bytes_accessed=4 * math.prod(shape), transcendentals=0
         ),
         name="pack_pages",
-    )(page_table.T, pool_kv)
+    )(in_hbm(page_table.T), in_hbm(pool_kv))
 
 
 def own_scores(rq, fresh_keys, tokens):
@@ -88,12 +99,12 @@
 
 def prepare_kernel(heads, factor, q_ref, cos_ref, sin_ref, keys_ref, values_ref,
                    rq_ref, state_ref):
-    tokens = q_ref.shape[1]
+    tokens = q_ref.shape[0]
     width = cos_ref.shape[1]
     rows = heads * tokens
     parts = []
     for h in range(heads):
-        x = q_ref[0, :, h * width:(h + 1) * width].astype(jnp.float32)
+        x = q_ref[:, h * width:(h + 1) * width].astype(jnp.float32)
         turned = pltpu.roll(x, width // 2, 1)
         parts.append((x * cos_ref[...] + turned * sin_ref[...]).astype(jnp.bfloat16))
     rq = jnp.concatenate(parts, axis=0)
@@ -101,56 +112,53 @@
     shift = jnp.max(own, axis=1, keepdims=True).astype(jnp.bfloat16).astype(jnp.float32)
     lane = lax.broadcasted_iota(jnp.int32, (rows, width), 1)
     extra = jnp.where(lane == 0, -shift, jnp.where(lane == 1, 1.0, 0.0))
-    rq_ref[0, :, :width] = rq
-    rq_ref[0, :, width:] = extra.astype(jnp.bfloat16)
+    rq_ref[:, :width] = rq
+    rq_ref[:, width:] = extra.astype(jnp.bfloat16)
     w = jnp.exp2((own - shift) * factor)
-    state_ref[0, :, :width] = lax.dot_general(
+    state_ref[:, :width] = lax.dot_general(
         w.astype(jnp.bfloat16), values_ref[...], CONTRACT_LAST,
         preferred_element_type=jnp.float32,
     )
-    state_ref[0, :, width:] = jnp.broadcast_to(jnp.sum(w, axis=1, keepdims=True), (rows, width))
+    state_ref[:, width:] = jnp.broadcast_to(jnp.sum(w, axis=1, keepdims=True), (rows, width))
 
 
 def prepare(q, cosine, sine, fresh_keys, fresh_values):
-    sets, tokens, wide = q.shape
+    tokens, wide = q.shape
     width, page = fresh_keys.shape
     heads = wide // width
     rows = heads * tokens
-    whole = lambda *shape: pl.BlockSpec(shape, lambda s: (0,) * len(shape))
-    each = lambda *shape: pl.BlockSpec((1,) + shape, lambda s: (s,) + (0,) * len(shape))
+    vmem = pl.BlockSpec(memory_space=pltpu.VMEM)
     return pl.pallas_call(
         functools.partial(prepare_kernel, heads, factor_of(width)),
-        grid=(sets,),
-        in_specs=[
-            each(tokens, wide),
-            whole(tokens, width),
-            whole(tokens, width),
-            whole(width, page),
-            whole(width, page),
-        ],
-        out_specs=[each(rows, 2 * width), each(rows, 2 * width)],
+        in_specs=[vmem] * 5,
+        out_specs=[vmem] * 2,
         out_shape=[
-            jax.ShapeDtypeStruct((sets, rows, 2 * width), jnp.bfloat16),
-            jax.ShapeDtypeStruct((sets, rows, 2 * width), jnp.float32),
+            jax.ShapeDtypeStruct((rows, 2 * width), jnp.bfloat16),
+            jax.ShapeDtypeStruct((rows, 2 * width), jnp.float32),
         ],
         compiler_params=pltpu.CompilerParams(vmem_limit_bytes=16 * MIB),
         cost_estimate=pl.CostEstimate(
-            flops=4 * sets * rows * page * width,
-            bytes_accessed=sets * rows * 2 * width * 6,
-            transcendentals=sets * rows * page,
+            flops=4 * rows * page * width,
+            bytes_accessed=rows * 2 * width * 6,
+            transcendentals=rows * page,
         ),
         name="prepare_queries",
     )(q, cosine, sine, fresh_keys, fresh_values)
 
 
-def attend_kernel(heads, factor, landing, live_ref, rq_ref, state_ref, all_ref, keys_ref,
+def attend_kernel(heads, factor, landing, live_ref, queries_ref, state_ref, all_ref, keys_ref,
                   values_ref, *refs):
     if landing:
-        landed_ref, whole_ref, placed_ref, acc_ref, top_ref, out_ref, sem = refs
-        place = pltpu.make_async_copy(landed_ref, placed_ref, sem.at[0])
+        landed_ref, out_ref, placed_ref, rq_ref, acc_ref, top_ref, sem = refs
+    else:
+        out_ref, rq_ref, acc_ref, top_ref, sem = refs
+    take_queries = pltpu.make_async_copy(queries_ref, rq_ref, sem.at[0])
+    take_queries.start()
+    take_state = pltpu.make_async_copy(state_ref, acc_ref, sem.at[1])
+    take_state.start()
+    if landing:
+        place = pltpu.make_async_copy(landed_ref, placed_ref, sem.at[2])
         place.start()
-    else:
-        out_ref, acc_ref, top_ref = refs
     tokens, wide = out_ref.shape
     width = wide // heads
     page = all_ref.shape[4]
@@ -165,12 +173,9 @@
         return jnp.concatenate([all_ref[p, 0, which], all_ref[p, 1, which]], axis=0)
 
     ones = jnp.ones((width, GROUPED * page), jnp.bfloat16)
-    acc_ref[...] = state_ref[int(landing)]
-    rq = rq_ref[int(landing)]
-
-    @pl.loop(0, pages // GROUPED, unroll=UNROLL)
-    def _(g):
-        at = g * GROUPED
+    take_queries.wait()
+    rq = rq_ref[...]
+    for at in range(0, pages, GROUPED):
         weights = []
         for i in range(0, GROUPED, 2):
             keys = jnp.concatenate(
@@ -183,6 +188,8 @@
             s = jnp.dot(rq, keys, preferred_element_type=jnp.float32)
             weights.append(jnp.exp2(s * factor).astype(jnp.bfloat16))
         values = jnp.concatenate([part_of(at + i, 1) for i in range(GROUPED)], axis=1)
+        if at == 0:
+            take_state.wait()
         acc_ref[...] += lax.dot_general(
             jnp.concatenate(weights, axis=1), jnp.concatenate([values, ones], axis=0),
             CONTRACT_LAST, preferred_element_type=jnp.float32,
@@ -190,16 +197,13 @@
 
     @pl.when(jnp.logical_not(jnp.max(acc_ref[:, width:]) <= 1e30))
     def _():
-        exact(factor, tokens, width, live_ref, rq_ref.at[int(landing)], keys_ref, values_ref,
+        exact(factor, tokens, width, live_ref, rq_ref, keys_ref, values_ref,
               all_ref, acc_ref, top_ref)
 
     done = (acc_ref[:, :width] / acc_ref[:, width:]).astype(jnp.bfloat16)
     for h in range(heads):
         out_ref[:, h * width:(h + 1) * width] = done[h * tokens:(h + 1) * tokens, :]
     if landing:
-        keep = pltpu.make_async_copy(out_ref, whole_ref.at[lax.axis_index("core")], sem.at[1])
-        keep.start()
-        keep.wait()
         place.wait()
 
 
@@ -243,7 +247,7 @@
 
 
 def attend(tokens, live, rq, state, arrived, fresh_keys, fresh_values, landed=None):
-    _, rows, double = rq.shape
+    rows, double = rq.shape
     pages, _, _, half, page = arrived.shape
     width = double // 2
     heads = rows // tokens
@@ -251,21 +255,21 @@
     landing = landed is not None
     vmem = pl.BlockSpec(memory_space=pltpu.VMEM)
     hbm = pl.BlockSpec(memory_space=pltpu.HBM)
-    scratch = [pltpu.VMEM((rows, double), jnp.float32), pltpu.VMEM((rows, page), jnp.float32)]
+    scratch = [
+        pltpu.VMEM((rows, double), jnp.bfloat16),
+        pltpu.VMEM((rows, double), jnp.float32),
+        pltpu.VMEM((rows, page), jnp.float32),
+        pltpu.SemaphoreType.DMA((3,)),
+    ]
+    more, more_specs = [], []
+    out_shape, out_specs = [jax.ShapeDtypeStruct(shape, jnp.bfloat16)], [vmem]
     if landing:
         more, more_specs = [landed], [vmem]
-        out_shape = [
-            jax.ShapeDtypeStruct((2,) + shape, jnp.bfloat16),
-            jax.ShapeDtypeStruct(landed.shape, landed.dtype),
-        ]
-        out_specs = [hbm, hbm]
-        scratch += [pltpu.VMEM(shape, jnp.bfloat16), pltpu.SemaphoreType.DMA((2,))]
-    else:
-        more, more_specs = [], []
-        out_shape, out_specs = jax.ShapeDtypeStruct(shape, jnp.bfloat16), vmem
+        out_shape.append(jax.ShapeDtypeStruct(landed.shape, landed.dtype))
+        out_specs.append(hbm)
     return pl.pallas_call(
         functools.partial(attend_kernel, heads, factor_of(width), landing),
-        in_specs=[pl.BlockSpec(memory_space=pltpu.SMEM)] + [vmem] * 5 + more_specs,
+        in_specs=[pl.BlockSpec(memory_space=pltpu.SMEM)] + [hbm] * 2 + [vmem] * 3 + more_specs,
         out_specs=out_specs,
         scratch_shapes=scratch,
         out_shape=out_shape,
@@ -276,7 +280,7 @@
             transcendentals=rows * pages * page,
         ),
         name="attend_kept" if landing else "attend_sent",
-    )(live, rq, state, arrived, fresh_keys, fresh_values, *more)
+    )(live, in_hbm(rq), in_hbm(state), arrived, fresh_keys, fresh_values, *more)
 
 
 def on_device(pool_kv, queries, new_kv, page_table, prefix_pages):
@@ -334,14 +338,18 @@
         jnp.concatenate([theirs, mine], axis=0),
     )
 
-    rq, state = prepare(
-        jnp.stack([taken, kept], axis=0), q_cosine, q_sine, fresh_keys, fresh_values
-    )
-    inputs = (live, rq, state, arrived, fresh_keys, fresh_values)
-    for_partner = attend(suffix_len, *inputs)
+    sent = prepare(taken, q_cosine, q_sine, fresh_keys, fresh_values)
+    kept = prepare(kept, q_cosine, q_sine, fresh_keys, fresh_values)
+    arrived, sent, kept = lax.optimization_barrier((arrived, sent, kept))
+    inputs = (arrived, fresh_keys, fresh_values)
+    (for_partner,) = attend(suffix_len, live, *sent, *inputs)
     from_partner = swap_cores(for_partner)
-    attended, landed = attend(suffix_len, *inputs, landed)
-    attended = lax.dynamic_update_index_in_dim(attended, from_partner, 1 - core, 0)
+    stays, landed = attend(suffix_len, live, *kept, *inputs, landed)
+    attended = jnp.where(
+        lower_half,
+        jnp.stack([stays, from_partner], axis=0),
+        jnp.stack([from_partner, stays], axis=0),
+    )
     return (attended, landed)
 
 

time: 82.3 us -> 81.9 us (level)
  Pallas kernels: 9.91 us -> 12.9 us
  waiting for transfers between devices: 33.9 us -> 31.8 us
  local copies, waits for them, and re-layouts: 5.13 us -> 3.33 us
    all_to_all x1, waiting for transfers between devices: 33.9 us -> 31.8 us  [on_device(): lax.all_to_all(pack(page_table, pool_kv), GROUP, split_axis=0, concat_axi...]
    pallas_call x2, Pallas kernels: 6.99 us -> 9 us  [attend(): pl.pallas_call(functools.partial(attend_kernel, heads, factor_of(width),...]
    unnamed x17, local copies, waits for them, and re-layouts: 4.17 us -> 3.05 us
    pallas_call x1, Pallas kernels: 1.91 us -> 2.88 us  [pack(): pl.pallas_call(pack_kernel, in_specs=[hbm, hbm], out_specs=hbm, scratch_s...]
  transfers between devices with their start and end apart: 5 -> 5, of which waited for: 1 -> 1; matrix products, arithmetic and copies ran while one was open for 2% -> 2% of each run, Pallas kernels for 10% -> 12%
where the time goes in v4:
time: 81.9 us; the launch traced here: 81.5 us
  waiting for transfers between devices  31.8 us (39%)
  starting transfers between devices  30.2 us (37%)
  Pallas kernels  12.9 us (16%)
  local copies, waits for them, and re-layouts  3.33 us (4%)
  other arithmetic  2.36 us (3%)
  between operations  0.96 us (1%)
    all_to_all x1, waiting for transfers between devices, on_device(): lax.all_to_all(pack(page_table, pool_kv), GROUP, split_axis=0, concat_axi...  31.8 us
    all_to_all x1, starting transfers between devices, on_device(): lax.all_to_all(pack(page_table, pool_kv), GROUP, split_axis=0, concat_axi...  15 us
    pallas_call x2, Pallas kernels, attend(): pl.pallas_call(functools.partial(attend_kernel, heads, factor_of(width),...  9 us
    ppermute x3, starting transfers between devices, swap_cores(): return lax.ppermute(array, 'core', [(0, 1), (1, 0)])  7.95 us
    ppermute x1, starting transfers between devices, from_behind(): lax.ppermute(array, axis, [(i, (i + by) % devices) for i in range(devices)])  7.3 us
    unnamed x17, local copies, waits for them, and re-layouts  3.05 us
    pallas_call x1, Pallas kernels, pack(): pl.pallas_call(pack_kernel, in_specs=[hbm, hbm], out_specs=hbm, scratch_s...  2.88 us
  transfers between devices with their start and end apart: 5, of which 1 were waited for; matrix products, arithmetic and copies ran while one was open for 2% of the time, Pallas kernels for 12%

profile of v4, /device:TPU:1, one launch (start us, length us, event | category | flops | bytes accessed | tf_op | source)
XLA Modules:
  0.0 81.5 jit_solution(6279646979956434558)
XLA Ops:
  0.6 2.9 %pack_pages.1 = bf16[64,2,64,128]{3,2,1,0:T(8,128)(2,1)} custom-call(s32[32,64]{1,0:T(8,128)} %bitcast.70, bf16[64,2,64,128]{3,2,1,0:T(8,128)(2,1)} %pool_ref.1), custom_call_target="tpu_custom_call" | custom-call | bytes 4194304 | tf_op jit(solution)/shard_map/pack_pages/pallas_call | solution.py:72
  3.5 0.0 copy-start.5
  3.5 0.0 copy-start.6
  3.5 0.0 copy-start.4
  3.6 0.0 copy-start.7
  3.6 15.0 %all-to-all-start = ((bf16[64,2,64,128]{3,2,1,0:T(8,128)(2,1)}), bf16[64,2,64,128]{3,2,1,0:T(8,128)(2,1)S(1)}, u32[]{:S(2)}, u32[]{:S(2)}) async-start(bf16[64,2,64,128]{3,2,1,0:T(8,128)(2,1)} %pack_pages.1), calls=%async_computation | async-start | bytes 4194304 | tf_op jit(solution)/shard_map/all_to_all | solution.py:295
  18.6 2.4 %collective-permute-start = (bf16[128,512]{1,0:T(8,128)(2,1)S(1)}, bf16[128,512]{1,0:T(8,128)(2,1)S(1)}, u32[]{:S(2)}, u32[]{:S(2)}) collective-permute-start(bf16[128,512]{1,0:T(8,128)(2,1)S(1)} %get-tuple-element.30), channel_id=1, source_target_pairs={{0,1},{1,0},{2,3},{3,2},{4,5},{5,4},{6,7},{7,6},{8,9},{9,8},{10,11... | collective-permute-start | bytes 393224 | tf_op jit(solution)/shard_map/ppermute | solution.py:27
  21.0 2.0 %collective-permute-start.1 = (bf16[2,2,64,128]{3,2,0,1:T(8,128)(2,1)S(1)}, bf16[2,2,64,128]{3,2,0,1:T(8,128)(2,1)S(1)}, u32[]{:S(2)}, u32[]{:S(2)}) collective-permute-start(bf16[2,2,64,128]{3,2,0,1:T(8,128)(2,1)S(1)} %copy.19), channel_id=1, source_target_pairs={{0,1},{1,0},{2,3},{3,2},{4,5},{5,4},{6,7},{7,6},{8,9},{9,8},{10,11... | collective-permute-start | bytes 196616 | tf_op jit(solution)/shard_map/ppermute | solution.py:27
  23.0 0.2 fusion.17
  23.2 0.1 fusion.19
  23.4 0.1 dynamic-slice_multiply_fusion
  23.5 0.1 add_convert_fusion
  23.5 0.1 broadcast_multiply_fusion
  23.6 0.2 cosine_bitcast_fusion
  23.9 0.2 fusion.21
  24.1 0.1 pad_maximum_fusion
  24.2 0.0 collective-permute-done.1
  24.3 0.3 bitcast_select_fusion
  24.6 7.3 %collective-permute-start.2 = (bf16[2,2,64,128]{3,2,1,0:T(8,128)(2,1)S(1)}, bf16[2,2,64,128]{3,2,1,0:T(8,128)(2,1)S(1)}, u32[]{:S(2)}, u32[]{:S(2)}) collective-permute-start(bf16[2,2,64,128]{3,2,1,0:T(8,128)(2,1)S(1)} %pad_maximum_fusion.2), channel_id=1, source_target_pairs={{0,256},{16,272},{32,288},{48,304},{64,320},{80,336},{96,352},{112... | collective-permute-start | bytes 196616 | tf_op jit(solution)/shard_map/ppermute | solution.py:32
  31.9 0.3 fusion.13
  32.3 0.5 prepare_queries.3
  32.8 0.8 copy-done
  33.6 0.7 copy-done.2
  34.3 0.0 collective-permute-done.q_ref
  34.3 0.5 prepare_queries.2
  34.8 0.8 copy-done.1
  35.6 0.7 copy-done.3
  36.3 31.8 %all-to-all-done = bf16[64,2,64,128]{3,2,1,0:T(8,128)(2,1)S(1)} async-done(((bf16[64,2,64,128]{3,2,1,0:T(8,128)(2,1)}), bf16[64,2,64,128]{3,2,1,0:T(8,128)(2,1)S(1)}, u32[]{:S(2)}, u32[]{:S(2)}) %all-to-all-start) | async-done | bytes 2097184 | tf_op jit(solution)/shard_map/all_to_all | solution.py:295
  68.1 4.5 %attend_sent.1 = bf16[128,512]{1,0:T(8,128)(2,1)S(1)} custom-call(s32[32]{0:T(128)S(1)} %convert_element_type.40.live_ref, bf16[512,256]{1,0:T(8,128)(2,1)} %copy-done.3, f32[512,256]{1,0:T(8,128)} %copy-done.1, bf16[32,2,2,64,128]{4,3,2,1,0:T(8,128)(2,1)S(1)} %bitcast.67, bf16[128,128]{1,0:T(8,128)(2,1)S(1)} %fusion.15.keys_ref, ...), custom_call_target="tpu_custom_call" | custom-call | flops 1073741824 | bytes 2097152 | tf_op jit(solution)/shard_map/attend_sent/pallas_call | solution.py:270
  72.6 3.6 %collective-permute-start.3 = (bf16[128,512]{1,0:T(8,128)(2,1)S(1)}, bf16[128,512]{1,0:T(8,128)(2,1)S(1)}, u32[]{:S(2)}, u32[]{:S(2)}) collective-permute-start(bf16[128,512]{1,0:T(8,128)(2,1)S(1)} %attend_sent.1), channel_id=1, source_target_pairs={{0,1},{1,0},{2,3},{3,2},{4,5},{5,4},{6,7},{7,6},{8,9},{9,8},{10,11... | collective-permute-start | bytes 393224 | tf_op jit(solution)/shard_map/ppermute | solution.py:27
  76.3 4.5 %attend_kept.1 = (bf16[128,512]{1,0:T(8,128)(2,1)S(1)}, bf16[2,2,64,128]{3,2,1,0:T(8,128)(2,1)}) custom-call(s32[32]{0:T(128)S(1)} %convert_element_type.40.live_ref, bf16[512,256]{1,0:T(8,128)(2,1)} %copy-done.2, f32[512,256]{1,0:T(8,128)} %copy-done, bf16[32,2,2,64,128]{4,3,2,1,0:T(8,128)(2,1)S(1)} %bitcast.68, bf16[128,128]{1,0:T(8,128)(2,1)S(1)} %fusion.15.keys_ref, ...), custom_call_target="tpu_custom_call" | custom-call | flops 1073741824 | bytes 2097152 | tf_op jit(solution)/shard_map/attend_kept/pallas_call | solution.py:270
  80.8 0.7 maximum_select_fusion
  (23 shorter events, 0.1 us)
Async XLA Ops:
  3.5 15.0 %copy-start.5 = (bf16[2,128,512]{2,1,0:T(8,128)(2,1)S(1)}, bf16[2,128,512]{2,1,0:T(8,128)(2,1)}, u32[]{:S(2)}) copy-start(bf16[2,128,512]{2,1,0:T(8,128)(2,1)} %param.6) | copy-start | bytes 786436
  3.5 17.4 %copy-start.6 = (bf16[2,2,64,128]{3,2,1,0:T(8,128)(2,1)S(1)}, bf16[2,2,64,128]{3,2,1,0:T(8,128)(2,1)}, u32[]{:S(2)}) copy-start(bf16[2,2,64,128]{3,2,1,0:T(8,128)(2,1)} %param.7) | copy-start | bytes 196612
  3.5 19.5 %copy-start.4 = (s32[64,32]{0,1:T(8,128)S(1)}, s32[64,32]{0,1:T(8,128)}, u32[]{:S(2)}) copy-start(s32[64,32]{0,1:T(8,128)} %param.8) | copy-start | bytes 24580
  3.6 19.8 %copy-start.7 = (s32[64]{0:T(128)S(1)}, s32[64]{0:T(128)}, u32[]{:S(2)}) copy-start(s32[64]{0:T(128)} %param.9) | copy-start | bytes 772
  3.6 64.5 %all-to-all-start = ((bf16[64,2,64,128]{3,2,1,0:T(8,128)(2,1)}), bf16[64,2,64,128]{3,2,1,0:T(8,128)(2,1)S(1)}, u32[]{:S(2)}, u32[]{:S(2)}) async-start(bf16[64,2,64,128]{3,2,1,0:T(8,128)(2,1)} %pack_pages.1), calls=%async_computation | async-start | bytes 4194304 | tf_op jit(solution)/shard_map/all_to_all | solution.py:295
  18.6 15.7 %collective-permute-start = (bf16[128,512]{1,0:T(8,128)(2,1)S(1)}, bf16[128,512]{1,0:T(8,128)(2,1)S(1)}, u32[]{:S(2)}, u32[]{:S(2)}) collective-permute-start(bf16[128,512]{1,0:T(8,128)(2,1)S(1)} %get-tuple-element.30), channel_id=1, source_target_pairs={{0,1},{1,0},{2,3},{3,2},{4,5},{5,4},{6,7},{7,6},{8,9},{9,8},{10,11... | collective-permute-start | bytes 393224 | tf_op jit(solution)/shard_map/ppermute | solution.py:27
  21.0 3.3 %collective-permute-start.1 = (bf16[2,2,64,128]{3,2,0,1:T(8,128)(2,1)S(1)}, bf16[2,2,64,128]{3,2,0,1:T(8,128)(2,1)S(1)}, u32[]{:S(2)}, u32[]{:S(2)}) collective-permute-start(bf16[2,2,64,128]{3,2,0,1:T(8,128)(2,1)S(1)} %copy.19), channel_id=1, source_target_pairs={{0,1},{1,0},{2,3},{3,2},{4,5},{5,4},{6,7},{7,6},{8,9},{9,8},{10,11... | collective-permute-start | bytes 196616 | tf_op jit(solution)/shard_map/ppermute | solution.py:27
  24.6 51.6 %collective-permute-start.2 = (bf16[2,2,64,128]{3,2,1,0:T(8,128)(2,1)S(1)}, bf16[2,2,64,128]{3,2,1,0:T(8,128)(2,1)S(1)}, u32[]{:S(2)}, u32[]{:S(2)}) collective-permute-start(bf16[2,2,64,128]{3,2,1,0:T(8,128)(2,1)S(1)} %pad_maximum_fusion.2), channel_id=1, source_target_pairs={{0,256},{16,272},{32,288},{48,304},{64,320},{80,336},{96,352},{112... | collective-permute-start | bytes 196616 | tf_op jit(solution)/shard_map/ppermute | solution.py:32
  32.8 0.8 %copy-start = (f32[512,256]{1,0:T(8,128)}, f32[512,256]{1,0:T(8,128)S(1)}, u32[]{:S(2)}) copy-start(f32[512,256]{1,0:T(8,128)S(1)} %get-tuple-element.18.state_ref) | copy-start | bytes 1572868
  33.6 0.7 copy-start.2
  34.8 0.8 copy-start.1
  35.6 0.7 copy-start.3
  72.6 8.2 %collective-permute-start.3 = (bf16[128,512]{1,0:T(8,128)(2,1)S(1)}, bf16[128,512]{1,0:T(8,128)(2,1)S(1)}, u32[]{:S(2)}, u32[]{:S(2)}) collective-permute-start(bf16[128,512]{1,0:T(8,128)(2,1)S(1)} %attend_sent.1), channel_id=1, source_target_pairs={{0,1},{1,0},{2,3},{3,2},{4,5},{5,4},{6,7},{7,6},{8,9},{9,8},{10,11... | collective-permute-start | bytes 393224 | tf_op jit(solution)/shard_map/ppermute | solution.py:27

commit v5 on v4

--- a/solution.py
+++ b/solution.py
@@ -13,14 +13,11 @@
 GROUP = ("pool", "core")
 CONTRACT_LAST = (((1,), (1,)), ((), ()))
 GROUPED = 8
+UNROLL = 4
 
 
 def factor_of(width):
     return math.log2(math.e) / math.sqrt(width)
-
-
-def in_hbm(array):
-    return pltpu.with_memory_space_constraint(array, pltpu.HBM)
 
 
 def swap_cores(array):
@@ -86,7 +83,10 @@
             flops=0, bytes_accessed=4 * math.prod(shape), transcendentals=0
         ),
         name="pack_pages",
-    )(in_hbm(page_table.T), in_hbm(pool_kv))
+    )(
+        pltpu.with_memory_space_constraint(page_table.T, pltpu.HBM),
+        pltpu.with_memory_space_constraint(pool_kv, pltpu.HBM),
+    )
 
 
 def own_scores(rq, fresh_keys, tokens):
@@ -97,8 +97,7 @@
     return jnp.where(key <= token, own, -1e30)
 
 
-def prepare_kernel(heads, factor, q_ref, cos_ref, sin_ref, keys_ref, values_ref,
-                   rq_ref, state_ref):
+def prepare_kernel(heads, q_ref, cos_ref, sin_ref, keys_ref, rq_ref):
     tokens = q_ref.shape[0]
     width = cos_ref.shape[1]
     rows = heads * tokens
@@ -114,51 +113,37 @@
     extra = jnp.where(lane == 0, -shift, jnp.where(lane == 1, 1.0, 0.0))
     rq_ref[:, :width] = rq
     rq_ref[:, width:] = extra.astype(jnp.bfloat16)
-    w = jnp.exp2((own - shift) * factor)
-    state_ref[:, :width] = lax.dot_general(
-        w.astype(jnp.bfloat16), values_ref[...], CONTRACT_LAST,
-        preferred_element_type=jnp.float32,
-    )
-    state_ref[:, width:] = jnp.broadcast_to(jnp.sum(w, axis=1, keepdims=True), (rows, width))
-
-
-def prepare(q, cosine, sine, fresh_keys, fresh_values):
+
+
+def prepare(q, cosine, sine, fresh_keys):
     tokens, wide = q.shape
     width, page = fresh_keys.shape
     heads = wide // width
     rows = heads * tokens
     vmem = pl.BlockSpec(memory_space=pltpu.VMEM)
     return pl.pallas_call(
-        functools.partial(prepare_kernel, heads, factor_of(width)),
-        in_specs=[vmem] * 5,
-        out_specs=[vmem] * 2,
-        out_shape=[
-            jax.ShapeDtypeStruct((rows, 2 * width), jnp.bfloat16),
-            jax.ShapeDtypeStruct((rows, 2 * width), jnp.float32),
-        ],
+        functools.partial(prepare_kernel, heads),
+        in_specs=[vmem] * 4,
+        out_specs=vmem,
+        out_shape=jax.ShapeDtypeStruct((rows, 2 * width), jnp.bfloat16),
         compiler_params=pltpu.CompilerParams(vmem_limit_bytes=16 * MIB),
         cost_estimate=pl.CostEstimate(
-            flops=4 * rows * page * width,
-            bytes_accessed=rows * 2 * width * 6,
-            transcendentals=rows * page,
+            flops=2 * rows * page * width,
+            bytes_accessed=rows * 2 * width * 2,
+            transcendentals=0,
         ),
         name="prepare_queries",
-    )(q, cosine, sine, fresh_keys, fresh_values)
-
-
-def attend_kernel(heads, factor, landing, live_ref, queries_ref, state_ref, all_ref, keys_ref,
+    )(q, cosine, sine, fresh_keys)
+
+
+def attend_kernel(heads, factor, landing, live_ref, rq_ref, all_ref, keys_ref,
                   values_ref, *refs):
     if landing:
-        landed_ref, out_ref, placed_ref, rq_ref, acc_ref, top_ref, sem = refs
+        landed_ref, out_ref, placed_ref, acc_ref, top_ref, sem = refs
+        place = pltpu.make_async_copy(landed_ref, placed_ref, sem)
+        place.start()
     else:
-        out_ref, rq_ref, acc_ref, top_ref, sem = refs
-    take_queries = pltpu.make_async_copy(queries_ref, rq_ref, sem.at[0])
-    take_queries.start()
-    take_state = pltpu.make_async_copy(state_ref, acc_ref, sem.at[1])
-    take_state.start()
-    if landing:
-        place = pltpu.make_async_copy(landed_ref, placed_ref, sem.at[2])
-        place.start()
+        out_ref, acc_ref, top_ref = refs
     tokens, wide = out_ref.shape
     width = wide // heads
     page = all_ref.shape[4]
@@ -173,9 +158,24 @@
         return jnp.concatenate([all_ref[p, 0, which], all_ref[p, 1, which]], axis=0)
 
     ones = jnp.ones((width, GROUPED * page), jnp.bfloat16)
-    take_queries.wait()
     rq = rq_ref[...]
-    for at in range(0, pages, GROUPED):
+    rows = rq.shape[0]
+    token = lax.rem(lax.broadcasted_iota(jnp.int32, (rows, page), 0), tokens)
+    key = lax.broadcasted_iota(jnp.int32, (rows, page), 1)
+    new_keys = jnp.concatenate(
+        [keys_ref[...], jnp.where(row == 0, 1.0, 0.0).astype(jnp.bfloat16)], axis=0
+    )
+    s = jnp.dot(rq, new_keys, preferred_element_type=jnp.float32)
+    w = jnp.exp2(jnp.where(key <= token, s, -1e30) * factor)
+    acc_ref[...] = lax.dot_general(
+        w.astype(jnp.bfloat16),
+        jnp.concatenate([values_ref[...], ones[:, :page]], axis=0),
+        CONTRACT_LAST, preferred_element_type=jnp.float32,
+    )
+
+    @pl.loop(0, pages // GROUPED, unroll=UNROLL)
+    def _(g):
+        at = g * GROUPED
         weights = []
         for i in range(0, GROUPED, 2):
             keys = jnp.concatenate(
@@ -188,8 +188,6 @@
             s = jnp.dot(rq, keys, preferred_element_type=jnp.float32)
             weights.append(jnp.exp2(s * factor).astype(jnp.bfloat16))
         values = jnp.concatenate([part_of(at + i, 1) for i in range(GROUPED)], axis=1)
-        if at == 0:
-            take_state.wait()
         acc_ref[...] += lax.dot_general(
             jnp.concatenate(weights, axis=1), jnp.concatenate([values, ones], axis=0),
             CONTRACT_LAST, preferred_element_type=jnp.float32,
@@ -246,7 +244,7 @@
         )
 
 
-def attend(tokens, live, rq, state, arrived, fresh_keys, fresh_values, landed=None):
+def attend(tokens, live, rq, arrived, fresh_keys, fresh_values, landed=None):
     rows, double = rq.shape
     pages, _, _, half, page = arrived.shape
     width = double // 2
@@ -254,22 +252,17 @@
     shape = (tokens, heads * width)
     landing = landed is not None
     vmem = pl.BlockSpec(memory_space=pltpu.VMEM)
-    hbm = pl.BlockSpec(memory_space=pltpu.HBM)
-    scratch = [
-        pltpu.VMEM((rows, double), jnp.bfloat16),
-        pltpu.VMEM((rows, double), jnp.float32),
-        pltpu.VMEM((rows, page), jnp.float32),
-        pltpu.SemaphoreType.DMA((3,)),
-    ]
+    scratch = [pltpu.VMEM((rows, double), jnp.float32), pltpu.VMEM((rows, page), jnp.float32)]
     more, more_specs = [], []
     out_shape, out_specs = [jax.ShapeDtypeStruct(shape, jnp.bfloat16)], [vmem]
     if landing:
         more, more_specs = [landed], [vmem]
         out_shape.append(jax.ShapeDtypeStruct(landed.shape, landed.dtype))
-        out_specs.append(hbm)
+        out_specs.append(pl.BlockSpec(memory_space=pltpu.HBM))
+        scratch.append(pltpu.SemaphoreType.DMA)
     return pl.pallas_call(
         functools.partial(attend_kernel, heads, factor_of(width), landing),
-        in_specs=[pl.BlockSpec(memory_space=pltpu.SMEM)] + [hbm] * 2 + [vmem] * 3 + more_specs,
+        in_specs=[pl.BlockSpec(memory_space=pltpu.SMEM)] + [vmem] * 4 + more_specs,
         out_specs=out_specs,
         scratch_shapes=scratch,
         out_shape=out_shape,
@@ -280,7 +273,7 @@
             transcendentals=rows * pages * page,
         ),
         name="attend_kept" if landing else "attend_sent",
-    )(live, in_hbm(rq), in_hbm(state), arrived, fresh_keys, fresh_values, *more)
+    )(live, rq, arrived, fresh_keys, fresh_values, *more)
 
 
 def on_device(pool_kv, queries, new_kv, page_table, prefix_pages):
@@ -338,13 +331,13 @@
         jnp.concatenate([theirs, mine], axis=0),
     )
 
-    sent = prepare(taken, q_cosine, q_sine, fresh_keys, fresh_values)
-    kept = prepare(kept, q_cosine, q_sine, fresh_keys, fresh_values)
+    sent = prepare(taken, q_cosine, q_sine, fresh_keys)
+    kept = prepare(kept, q_cosine, q_sine, fresh_keys)
     arrived, sent, kept = lax.optimization_barrier((arrived, sent, kept))
     inputs = (arrived, fresh_keys, fresh_values)
-    (for_partner,) = attend(suffix_len, live, *sent, *inputs)
+    (for_partner,) = attend(suffix_len, live, sent, *inputs)
     from_partner = swap_cores(for_partner)
-    stays, landed = attend(suffix_len, live, *kept, *inputs, landed)
+    stays, landed = attend(suffix_len, live, kept, *inputs, landed)
     attended = jnp.where(
         lower_half,
         jnp.stack([stays, from_partner], axis=0),

time: 81.9 us -> 79.7 us (0.973)
  waiting for transfers between devices: 31.8 us -> 35.1 us
  local copies, waits for them, and re-layouts: 3.33 us -> 0.31 us
  Pallas kernels: 12.9 us -> 10.5 us
    all_to_all x1, waiting for transfers between devices: 31.8 us -> 35.1 us  [on_device(): lax.all_to_all(pack(page_table, pool_kv), GROUP, split_axis=0, concat_axi...]
    unnamed x17 -> x9, local copies, waits for them, and re-layouts: 3.05 us -> 0.03 us
    pallas_call x2, Pallas kernels: 9 us -> 6.87 us  [attend(): pl.pallas_call(functools.partial(attend_kernel, heads, factor_of(width),...]
  transfers between devices with their start and end apart: 5 -> 5, of which waited for: 1 -> 1; matrix products, arithmetic and copies ran while one was open for 2% -> 2% of each run, Pallas kernels for 12% -> 10%
where the time goes in v5:
time: 79.7 us; the launch traced here: 79.4 us
  waiting for transfers between devices  35.1 us (44%)
  starting transfers between devices  30.2 us (38%)
  Pallas kernels  10.5 us (13%)
  other arithmetic  2.35 us (3%)
  between operations  0.96 us (1%)
    all_to_all x1, waiting for transfers between devices, on_device(): lax.all_to_all(pack(page_table, pool_kv), GROUP, split_axis=0, concat_axi...  35.1 us
    all_to_all x1, starting transfers between devices, on_device(): lax.all_to_all(pack(page_table, pool_kv), GROUP, split_axis=0, concat_axi...  15 us
    ppermute x3, starting transfers between devices, swap_cores(): return lax.ppermute(array, 'core', [(0, 1), (1, 0)])  7.95 us
    ppermute x1, starting transfers between devices, from_behind(): lax.ppermute(array, axis, [(i, (i + by) % devices) for i in range(devices)])  7.3 us
    pallas_call x2, Pallas kernels, attend(): pl.pallas_call(functools.partial(attend_kernel, heads, factor_of(width),...  6.87 us
    pallas_call x1, Pallas kernels, pack(): pl.pallas_call(pack_kernel, in_specs=[hbm, hbm], out_specs=hbm, scratch_s...  2.89 us
  transfers between devices with their start and end apart: 5, of which 1 were waited for; matrix products, arithmetic and copies ran while one was open for 2% of the time, Pallas kernels for 10%

profile of v5, /device:TPU:1, one launch (start us, length us, event | category | flops | bytes accessed | tf_op | source)
XLA Modules:
  0.0 79.4 jit_solution(9864412843614425348)
XLA Ops:
  0.6 2.9 %pack_pages.1 = bf16[64,2,64,128]{3,2,1,0:T(8,128)(2,1)} custom-call(s32[32,64]{1,0:T(8,128)} %bitcast.70, bf16[64,2,64,128]{3,2,1,0:T(8,128)(2,1)} %pool_ref.1), custom_call_target="tpu_custom_call" | custom-call | bytes 4194304 | tf_op jit(solution)/shard_map/pack_pages/pallas_call | solution.py:69
  3.5 0.0 copy-start.1
  3.5 0.0 copy-start.2
  3.5 0.0 copy-start
  3.6 0.0 copy-start.3
  3.6 15.0 %all-to-all-start = ((bf16[64,2,64,128]{3,2,1,0:T(8,128)(2,1)}), bf16[64,2,64,128]{3,2,1,0:T(8,128)(2,1)S(1)}, u32[]{:S(2)}, u32[]{:S(2)}) async-start(bf16[64,2,64,128]{3,2,1,0:T(8,128)(2,1)} %pack_pages.1), calls=%async_computation | async-start | bytes 4194304 | tf_op jit(solution)/shard_map/all_to_all | solution.py:288
  18.6 0.0 copy-done.1
  18.6 2.4 %collective-permute-start = (bf16[128,512]{1,0:T(8,128)(2,1)S(1)}, bf16[128,512]{1,0:T(8,128)(2,1)S(1)}, u32[]{:S(2)}, u32[]{:S(2)}) collective-permute-start(bf16[128,512]{1,0:T(8,128)(2,1)S(1)} %get-tuple-element.18), channel_id=1, source_target_pairs={{0,1},{1,0},{2,3},{3,2},{4,5},{5,4},{6,7},{7,6},{8,9},{9,8},{10,11... | collective-permute-start | bytes 393224 | tf_op jit(solution)/shard_map/ppermute | solution.py:24
  21.0 2.0 %collective-permute-start.1 = (bf16[2,2,64,128]{3,2,0,1:T(8,128)(2,1)S(1)}, bf16[2,2,64,128]{3,2,0,1:T(8,128)(2,1)S(1)}, u32[]{:S(2)}, u32[]{:S(2)}) collective-permute-start(bf16[2,2,64,128]{3,2,0,1:T(8,128)(2,1)S(1)} %copy.19), channel_id=1, source_target_pairs={{0,1},{1,0},{2,3},{3,2},{4,5},{5,4},{6,7},{7,6},{8,9},{9,8},{10,11... | collective-permute-start | bytes 196616 | tf_op jit(solution)/shard_map/ppermute | solution.py:24
  23.0 0.2 fusion.17
  23.2 0.1 fusion.19
  23.4 0.0 copy-done.3
  23.4 0.1 dynamic-slice_multiply_fusion
  23.5 0.1 add_convert_fusion
  23.5 0.1 broadcast_multiply_fusion
  23.6 0.2 cosine_bitcast_fusion
  23.9 0.2 fusion.21
  24.1 0.1 pad_maximum_fusion
  24.2 0.0 collective-permute-done.1
  24.3 0.3 bitcast_select_fusion
  24.6 7.3 %collective-permute-start.2 = (bf16[2,2,64,128]{3,2,1,0:T(8,128)(2,1)S(1)}, bf16[2,2,64,128]{3,2,1,0:T(8,128)(2,1)S(1)}, u32[]{:S(2)}, u32[]{:S(2)}) collective-permute-start(bf16[2,2,64,128]{3,2,1,0:T(8,128)(2,1)S(1)} %pad_maximum_fusion.2), channel_id=1, source_target_pairs={{0,256},{16,272},{32,288},{48,304},{64,320},{80,336},{96,352},{112... | collective-permute-start | bytes 196616 | tf_op jit(solution)/shard_map/ppermute | solution.py:29
  32.0 0.3 fusion.13
  32.3 0.3 prepare_queries.3.rq_ref
  32.7 0.0 collective-permute-done.q_ref
  32.7 0.3 prepare_queries.2.rq_ref
  33.0 35.1 %all-to-all-done = bf16[64,2,64,128]{3,2,1,0:T(8,128)(2,1)S(1)} async-done(((bf16[64,2,64,128]{3,2,1,0:T(8,128)(2,1)}), bf16[64,2,64,128]{3,2,1,0:T(8,128)(2,1)S(1)}, u32[]{:S(2)}, u32[]{:S(2)}) %all-to-all-start) | async-done | bytes 2097184 | tf_op jit(solution)/shard_map/all_to_all | solution.py:288
  68.1 3.4 %attend_sent.1 = bf16[128,512]{1,0:T(8,128)(2,1)S(1)} custom-call(s32[32]{0:T(128)S(1)} %convert_element_type.40.live_ref, bf16[512,256]{1,0:T(8,128)(2,1)S(1)} %prepare_queries.2.rq_ref, bf16[32,2,2,64,128]{4,3,2,1,0:T(8,128)(2,1)S(1)} %bitcast.67, bf16[128,128]{1,0:T(8,128)(2,1)S(1)} %fusion.15.keys_ref, bf16[128,128]{1,0:T(8,128)(2,1)S(1)} %maximum_select_fusion.1.values_ref), custom_call_target="tpu_custom_call" | custom-call | flops 1073741824 | bytes 2097152 | tf_op jit(solution)/shard_map/attend_sent/pallas_call | solution.py:263
  71.6 3.6 %collective-permute-start.3 = (bf16[128,512]{1,0:T(8,128)(2,1)S(1)}, bf16[128,512]{1,0:T(8,128)(2,1)S(1)}, u32[]{:S(2)}, u32[]{:S(2)}) collective-permute-start(bf16[128,512]{1,0:T(8,128)(2,1)S(1)} %attend_sent.1), channel_id=1, source_target_pairs={{0,1},{1,0},{2,3},{3,2},{4,5},{5,4},{6,7},{7,6},{8,9},{9,8},{10,11... | collective-permute-start | bytes 393224 | tf_op jit(solution)/shard_map/ppermute | solution.py:24
  75.2 0.0 collective-permute-done.2.refs_0_
  75.2 3.4 %attend_kept.1 = (bf16[128,512]{1,0:T(8,128)(2,1)S(1)}, bf16[2,2,64,128]{3,2,1,0:T(8,128)(2,1)}) custom-call(s32[32]{0:T(128)S(1)} %convert_element_type.40.live_ref, bf16[512,256]{1,0:T(8,128)(2,1)S(1)} %prepare_queries.3.rq_ref, bf16[32,2,2,64,128]{4,3,2,1,0:T(8,128)(2,1)S(1)} %bitcast.68, bf16[128,128]{1,0:T(8,128)(2,1)S(1)} %fusion.15.keys_ref, ...), custom_call_target="tpu_custom_call" | custom-call | flops 1073741824 | bytes 2097152 | tf_op jit(solution)/shard_map/attend_kept/pallas_call | solution.py:263
  78.7 0.0 collective-permute-done.3
  78.7 0.7 maximum_select_fusion
  (15 shorter events, 0.1 us)
Async XLA Ops:
  3.5 15.0 %copy-start.1 = (bf16[2,128,512]{2,1,0:T(8,128)(2,1)S(1)}, bf16[2,128,512]{2,1,0:T(8,128)(2,1)}, u32[]{:S(2)}) copy-start(bf16[2,128,512]{2,1,0:T(8,128)(2,1)} %param.6) | copy-start | bytes 786436
  3.5 17.4 %copy-start.2 = (bf16[2,2,64,128]{3,2,1,0:T(8,128)(2,1)S(1)}, bf16[2,2,64,128]{3,2,1,0:T(8,128)(2,1)}, u32[]{:S(2)}) copy-start(bf16[2,2,64,128]{3,2,1,0:T(8,128)(2,1)} %param.7) | copy-start | bytes 196612
  3.5 19.5 %copy-start = (s32[64,32]{0,1:T(8,128)S(1)}, s32[64,32]{0,1:T(8,128)}, u32[]{:S(2)}) copy-start(s32[64,32]{0,1:T(8,128)} %param.8) | copy-start | bytes 24580
  3.6 19.8 %copy-start.3 = (s32[64]{0:T(128)S(1)}, s32[64]{0:T(128)}, u32[]{:S(2)}) copy-start(s32[64]{0:T(128)} %param.9) | copy-start | bytes 772
  3.6 64.5 %all-to-all-start = ((bf16[64,2,64,128]{3,2,1,0:T(8,128)(2,1)}), bf16[64,2,64,128]{3,2,1,0:T(8,128)(2,1)S(1)}, u32[]{:S(2)}, u32[]{:S(2)}) async-start(bf16[64,2,64,128]{3,2,1,0:T(8,128)(2,1)} %pack_pages.1), calls=%async_computation | async-start | bytes 4194304 | tf_op jit(solution)/shard_map/all_to_all | solution.py:288
  18.6 14.1 %collective-permute-start = (bf16[128,512]{1,0:T(8,128)(2,1)S(1)}, bf16[128,512]{1,0:T(8,128)(2,1)S(1)}, u32[]{:S(2)}, u32[]{:S(2)}) collective-permute-start(bf16[128,512]{1,0:T(8,128)(2,1)S(1)} %get-tuple-element.18), channel_id=1, source_target_pairs={{0,1},{1,0},{2,3},{3,2},{4,5},{5,4},{6,7},{7,6},{8,9},{9,8},{10,11... | collective-permute-start | bytes 393224 | tf_op jit(solution)/shard_map/ppermute | solution.py:24
  21.0 3.2 %collective-permute-start.1 = (bf16[2,2,64,128]{3,2,0,1:T(8,128)(2,1)S(1)}, bf16[2,2,64,128]{3,2,0,1:T(8,128)(2,1)S(1)}, u32[]{:S(2)}, u32[]{:S(2)}) collective-permute-start(bf16[2,2,64,128]{3,2,0,1:T(8,128)(2,1)S(1)} %copy.19), channel_id=1, source_target_pairs={{0,1},{1,0},{2,3},{3,2},{4,5},{5,4},{6,7},{7,6},{8,9},{9,8},{10,11... | collective-permute-start | bytes 196616 | tf_op jit(solution)/shard_map/ppermute | solution.py:24
  24.6 50.6 %collective-permute-start.2 = (bf16[2,2,64,128]{3,2,1,0:T(8,128)(2,1)S(1)}, bf16[2,2,64,128]{3,2,1,0:T(8,128)(2,1)S(1)}, u32[]{:S(2)}, u32[]{:S(2)}) collective-permute-start(bf16[2,2,64,128]{3,2,1,0:T(8,128)(2,1)S(1)} %pad_maximum_fusion.2), channel_id=1, source_target_pairs={{0,256},{16,272},{32,288},{48,304},{64,320},{80,336},{96,352},{112... | collective-permute-start | bytes 196616 | tf_op jit(solution)/shard_map/ppermute | solution.py:29
  71.6 7.1 %collective-permute-start.3 = (bf16[128,512]{1,0:T(8,128)(2,1)S(1)}, bf16[128,512]{1,0:T(8,128)(2,1)S(1)}, u32[]{:S(2)}, u32[]{:S(2)}) collective-permute-start(bf16[128,512]{1,0:T(8,128)(2,1)S(1)} %attend_sent.1), channel_id=1, source_target_pairs={{0,1},{1,0},{2,3},{3,2},{4,5},{5,4},{6,7},{7,6},{8,9},{9,8},{10,11... | collective-permute-start | bytes 393224 | tf_op jit(solution)/shard_map/ppermute | solution.py:24
